TPU v7x, 32 devices: a whole 2x2x4 slice. The times are simulated.
32 devices in a mesh: seq: 8 (over z, y), head: 4 (over x, core).
Axes of the slice: x: 2, y: 2, z: 4, core: 2. Of those that a mesh axis runs over, the one named last changes fastest.
Arguments:
- node_features: bfloat16 [12288, 512], P('seq'), may hold values from -136 to 136
- gain: float32 [512], replicated, may hold values from 0.5 to 1.5
- w_qkv: bfloat16 [3, 512, 512], P(None, None, 'head'), may hold values from -3.1 to 3.1
- d_out: bfloat16 [12288, 512], P('seq'), may hold values from -6 to 6
- pattern: int32 [96, 3], replicated, may hold values from 0 to 95, as said below
- counts: int32 [96], P('seq'), may hold values from 1 to 3
Outputs:
- layer_output: bfloat16 [12288, 512], P('seq', 'head')
- grad_input: bfloat16 [12288, 512], P('seq', 'head')
- grad_weights: float32 [3, 512, 512], P(None, 'seq', 'head')
Inputs may be any that keep to these rules, and one draw needn't show every extreme that they name: `pattern`: block id p lives on index p // 12 of seq. Among the 36 entries of the query blocks of one index of seq (live or not), at most 6 name blocks living on any one index of seq, and on every index some index is named exactly 6 times.
All inputs are finite; a program needn't handle non-finite values.
Results may differ from a plain program's by a relative error of at most 0.012.
The roundings to bfloat16 on the way count: a program that leaves them out, or rounds other values in their place, can miss the bound.
Values may be sent and summed in bfloat16 or wider, within the bound.
A program may use at most 128 MiB of HBM per device.

v0:
```python
import math

import jax
import jax.numpy as jnp
from jax import lax
from jax.sharding import PartitionSpec as P

HEAD_DIM = 64
BLOCK = 128
EXPD = 3


EPS = 1e-06


def shards(node_features, gain, w_qkv, d_out, pattern, counts):
    seq_count = lax.axis_size("seq")
    my_index = lax.axis_index("seq")
    row_count = node_features.shape[0]
    block_count = row_count // BLOCK
    col_count = w_qkv.shape[2]
    heads_here = col_count // HEAD_DIM
    slot_count = block_count * EXPD
    capacity = max(2, 3 * slot_count // (2 * seq_count))
    kv_width = 2 * col_count
    score_scale = 1.0 / math.sqrt(HEAD_DIM)
    col_start = lax.axis_index("head") * col_count
    x_float = node_features.astype(jnp.float32)
    inv_rms = lax.rsqrt(jnp.mean(x_float * x_float, axis=1, keepdims=True) + EPS)
    normed = (x_float * inv_rms * gain).astype(jnp.bfloat16)
    queries = jnp.dot(normed, w_qkv[0], preferred_element_type=jnp.float32).astype(jnp.bfloat16)
    keys_here = jnp.dot(normed, w_qkv[1], preferred_element_type=jnp.float32).astype(jnp.bfloat16)
    values_here = jnp.dot(normed, w_qkv[2], preferred_element_type=jnp.float32).astype(jnp.bfloat16)
    kv_local = jnp.stack(
        [
            keys_here.reshape(row_count, heads_here, HEAD_DIM),
            values_here.reshape(row_count, heads_here, HEAD_DIM),
        ],
        axis=2,
    )
    kv_local = kv_local.reshape(block_count, BLOCK, kv_width)
    owners = (pattern // block_count).reshape(seq_count, slot_count)
    in_owner = (pattern % block_count).reshape(seq_count, slot_count)
    peers = jnp.arange(seq_count, dtype=jnp.int32)
    places = jnp.arange(capacity, dtype=jnp.int32)
    hits = (owners[:, :, None] == peers[None, None, :]).astype(jnp.int32)
    ranks = jnp.sum((jnp.cumsum(hits, axis=1) - hits) * hits, axis=2)
    picked = (owners[:, None, :] == my_index) & (ranks[:, None, :] == places[None, :, None])
    sent_from = jnp.sum(jnp.where(picked, in_owner[:, None, :], 0), axis=2)
    filled = jnp.any(picked, axis=2)
    outgoing = jnp.where(filled[:, :, None, None], kv_local[sent_from], jnp.zeros((), jnp.bfloat16))
    incoming = lax.all_to_all(outgoing, "seq", split_axis=0, concat_axis=0, tiled=True)
    my_owners = lax.dynamic_index_in_dim(owners, my_index, 0, keepdims=False)
    my_ranks = lax.dynamic_index_in_dim(ranks, my_index, 0, keepdims=False)
    slot_kv = incoming.reshape(seq_count * capacity, BLOCK, kv_width)[
        my_owners * capacity + my_ranks
    ]
    gathered = jnp.concatenate(
        [kv_local[:, None], slot_kv.reshape(block_count, EXPD, BLOCK, kv_width)], axis=1
    )
    gathered = gathered.reshape(block_count, 1 + EXPD, BLOCK, heads_here, 2, HEAD_DIM)
    key_side = gathered[:, :, :, :, 0, :]
    value_side = gathered[:, :, :, :, 1, :]
    live = jnp.concatenate(
        [jnp.ones((block_count, 1), bool), jnp.arange(EXPD)[None, :] < counts[:, None]], axis=1
    )
    query_blocks = queries.reshape(block_count, BLOCK, heads_here, HEAD_DIM)
    scores = (
        jnp.einsum("bqhe,btkhe->bhqtk", query_blocks, key_side, preferred_element_type=jnp.float32)
        * score_scale
    )
    scores = jnp.where(live[:, None, None, :, None], scores, -jnp.inf)
    row_peak = jnp.max(scores, axis=(3, 4), keepdims=True)
    powers = jnp.exp(scores - row_peak)
    attention = powers / jnp.sum(powers, axis=(3, 4), keepdims=True)
    attention_low = attention.astype(jnp.bfloat16)
    attended = jnp.einsum(
        "bhqtk,btkhe->bqhe", attention_low, value_side, preferred_element_type=jnp.float32
    )
    x_mine = lax.dynamic_slice_in_dim(x_float, col_start, col_count, 1)
    layer_output = (x_mine + attended.reshape(row_count, col_count)).astype(jnp.bfloat16)
    grad_mine_out = lax.dynamic_slice_in_dim(d_out, col_start, col_count, 1)
    grad_blocks = grad_mine_out.reshape(block_count, BLOCK, heads_here, HEAD_DIM)
    grad_attention = jnp.einsum(
        "bqhe,btkhe->bhqtk", grad_blocks, value_side, preferred_element_type=jnp.float32
    )
    row_dot = jnp.transpose(jnp.sum(grad_blocks.astype(jnp.float32) * attended, axis=3), (0, 2, 1))
    grad_scores = (
        attention * (grad_attention - row_dot[:, :, :, None, None]) * score_scale
    ).astype(jnp.bfloat16)
    grad_queries = jnp.einsum(
        "bhqtk,btkhe->bqhe", grad_scores, key_side, preferred_element_type=jnp.float32
    )
    grad_queries = grad_queries.astype(jnp.bfloat16).reshape(row_count, col_count)
    grad_key_terms = jnp.einsum(
        "bhqtk,bqhe->btkhe", grad_scores, query_blocks, preferred_element_type=jnp.float32
    )
    grad_value_terms = jnp.einsum(
        "bhqtk,bqhe->btkhe", attention_low, grad_blocks, preferred_element_type=jnp.float32
    )
    contrib = jnp.stack([grad_key_terms, grad_value_terms], axis=4).reshape(
        block_count, 1 + EXPD, BLOCK, kv_width
    )
    remote = contrib[:, 1:].reshape(slot_count, BLOCK, kv_width)
    slot_ids = jnp.arange(slot_count, dtype=jnp.int32)
    back_pick = (my_owners[None, None, :] == peers[:, None, None]) & (
        my_ranks[None, None, :] == places[None, :, None]
    )
    back_from = jnp.sum(jnp.where(back_pick, slot_ids[None, None, :], 0), axis=2)
    back_fill = jnp.any(back_pick, axis=2)
    returning = jnp.where(
        back_fill[:, :, None, None], remote[back_from], jnp.zeros((), jnp.float32)
    )
    returned = lax.all_to_all(returning, "seq", split_axis=0, concat_axis=0, tiled=True)
    owned = (
        (sent_from.reshape(-1)[None, :] == jnp.arange(block_count, dtype=jnp.int32)[:, None])
        & filled.reshape(-1)[None, :]
    ).astype(jnp.float32)
    added = jnp.dot(
        owned,
        returned.reshape(seq_count * capacity, BLOCK * kv_width),
        precision=lax.Precision.HIGHEST,
        preferred_element_type=jnp.float32,
    )
    grad_total = (contrib[:, 0].reshape(block_count, BLOCK * kv_width) + added).reshape(
        row_count, heads_here, 2, HEAD_DIM
    )
    grad_keys = grad_total[:, :, 0, :].reshape(row_count, col_count).astype(jnp.bfloat16)
    grad_values = grad_total[:, :, 1, :].reshape(row_count, col_count).astype(jnp.bfloat16)
    grads = (grad_queries, grad_keys, grad_values)
    contract_cols = (((1,), (1,)), ((), ()))
    grad_normed = lax.dot_general(
        grad_queries, w_qkv[0], contract_cols, preferred_element_type=jnp.float32
    )
    grad_normed = grad_normed + lax.dot_general(
        grad_keys, w_qkv[1], contract_cols, preferred_element_type=jnp.float32
    )
    grad_normed = grad_normed + lax.dot_general(
        grad_values, w_qkv[2], contract_cols, preferred_element_type=jnp.float32
    )
    gain_mine = lax.dynamic_slice_in_dim(gain, col_start, col_count, 0)
    summed = lax.psum(grad_normed.astype(jnp.bfloat16), "head").astype(jnp.float32)
    row_term = jnp.mean(x_float * gain * summed, axis=1, keepdims=True)
    grad_cols = lax.dynamic_slice_in_dim(summed, col_start, col_count, 1)
    cubed = inv_rms * inv_rms * inv_rms
    grad_input = (
        grad_mine_out.astype(jnp.float32)
        + inv_rms * gain_mine * grad_cols
        - x_mine * cubed * row_term
    ).astype(jnp.bfloat16)
    node_count = row_count * seq_count
    contract_rows = (((0,), (0,)), ((), ()))
    terms = jnp.stack(
        [
            lax.dot_general(normed, member, contract_rows, preferred_element_type=jnp.float32)
            for member in grads
        ]
    ) / math.sqrt(node_count)
    grad_weights = lax.psum_scatter(
        terms.astype(jnp.bfloat16), "seq", scatter_dimension=1, tiled=True
    ).astype(jnp.float32)
    return (layer_output, grad_input, grad_weights)


def solution(mesh):
    in_specs = (P("seq", None), P(), P(None, None, "head"), P("seq", None), P(), P("seq"))
    out_specs = (P("seq", "head"), P("seq", "head"), P(None, "seq", "head"))
    return jax.shard_map(shards, mesh=mesh, in_specs=in_specs, out_specs=out_specs, check_vma=False)
```

profile of v0, /device:TPU:0, one launch (start us, length us, event | category | flops | bytes accessed | tf_op | source)
XLA Modules:
  0.0 409.1 jit_solution(9188604645811607008)
XLA Ops:
  17.3 2.5 gather_fusion
  19.9 3.9 broadcast_select_fusion.1
  23.7 7.6 %all-to-all-start = ((bf16[8,6,128,256]{3,2,1,0:T(8,128)(2,1)}), bf16[8,6,128,256]{3,2,1,0:T(8,128)(2,1)}, u32[]{:S(2)}, u32[]{:S(2)}) async-start(bf16[8,6,128,256]{3,2,1,0:T(8,128)(2,1)} %broadcast_select_fusion.1), calls=%async_computation | async-start | bytes 6291456 | tf_op jit(solution)/shard_map/all_to_all | solution.py:52
  38.3 63.8 %all-to-all-done = bf16[8,6,128,256]{3,2,1,0:T(8,128)(2,1)} async-done(((bf16[8,6,128,256]{3,2,1,0:T(8,128)(2,1)}), bf16[8,6,128,256]{3,2,1,0:T(8,128)(2,1)}, u32[]{:S(2)}, u32[]{:S(2)}) %all-to-all-start) | async-done | bytes 3145760 | tf_op jit(solution)/shard_map/all_to_all | solution.py:52
  102.1 4.2 %gather_fusion.1 = bf16[36,128,256]{2,1,0:T(8,128)(2,1)} fusion(bf16[48,128,256]{2,1,0:T(8,128)(2,1)} %bitcast.8, s32[1024]{0:T(1024)S(1)} %pad_clamp_fusion.1), kind=kCustom, calls=%fused_computation.1 | custom fusion | bytes 4718736 | tf_op jit(solution)/shard_map/gather | solution.py:55
  106.3 4.3 %copy.191 = bf16[36,128,256]{1,2,0:T(8,128)(2,1)} copy(bf16[36,128,256]{2,1,0:T(8,128)(2,1)} %gather_fusion.1) | data formatting | bytes 4718592 | tf_op jit(solution)/shard_map/gather | solution.py:55
  115.8 3.0 multiply_reduce_fusion.2
  120.9 3.5 multiply_convert_fusion
  129.5 2.6 copy-done
  132.1 2.5 slice.48
  134.6 6.0 %copy.213 = f32[12,3,128,256]{3,2,1,0:T(8,128)} copy(f32[12,3,128,256]{2,3,1,0:T(8,128)} %slice.48) | data formatting | bytes 9437184 | tf_op jit(solution)/shard_map/slice | solution.py:104
  140.6 5.9 %gather_fusion.2 = f32[48,128,256]{2,1,0:T(8,128)} fusion(f32[36,128,256]{2,1,0:T(8,128)} %bitcast.137, s32[1024]{0:T(1024)S(1)} %pad_clamp_fusion), kind=kCustom, calls=%fused_computation.2 | custom fusion | bytes 12583104 | tf_op jit(solution)/shard_map/gather | solution.py:112
  146.5 6.6 %broadcast_select_fusion = f32[8,6,128,256]{3,2,1,0:T(8,128)} fusion(f32[8,6,128,256]{3,2,1,0:T(8,128)} %bitcast.141, pred[8,6]{1,0:T(8,128)(4,1)S(1)} %copy.212), kind=kLoop, calls=%fused_computation.15 | loop fusion | flops 1572864 | bytes 12582960 | tf_op jit(solution)/shard_map/jit(_where)/select_n | solution.py:111
  153.1 4.8 %all-to-all-start.1 = ((f32[8,6,128,256]{3,2,1,0:T(8,128)}), f32[8,6,128,256]{3,2,1,0:T(8,128)}, u32[]{:S(2)}, u32[]{:S(2)}) async-start(f32[8,6,128,256]{3,2,1,0:T(8,128)} %broadcast_select_fusion), calls=%async_computation.1 | async-start | bytes 12582912 | tf_op jit(solution)/shard_map/all_to_all | solution.py:114
  160.5 2.6 fusion.14
  167.5 2.5 copy.241
  170.1 3.2 fusion.18
  173.2 122.0 %all-to-all-done.1 = f32[8,6,128,256]{3,2,1,0:T(8,128)} async-done(((f32[8,6,128,256]{3,2,1,0:T(8,128)}), f32[8,6,128,256]{3,2,1,0:T(8,128)}, u32[]{:S(2)}, u32[]{:S(2)}) %all-to-all-start.1) | async-done | bytes 6291488 | tf_op jit(solution)/shard_map/all_to_all | solution.py:114
  295.2 6.5 %copy.242 = f32[6,8,128,256]{3,1,2,0:T(8,128)S(1)} copy(f32[6,8,128,256]{3,2,1,0:T(8,128)} %bitcast.64) | data formatting | bytes 12582912
  301.7 3.4 convolution_add_fusion
  305.1 3.8 reshape.206
  309.0 3.5 fusion.51
  312.4 3.4 copy.238
  315.8 3.5 copy.239
  319.4 2.6 convolution_add_fusion.2
  322.0 2.8 fusion.3
  328.2 3.3 copy.230
  331.5 3.1 reshape.239
  338.4 28.4 %all-reduce.3.cloned.1.call-done = bf16[1536,512]{1,0:T(8,128)(2,1)} async-done(((bf16[1536,512]{1,0:T(8,128)(2,1)}), bf16[1536,512]{1,0:T(8,128)(2,1)}) %all-reduce.3.cloned.1.call-update) | async-done | bytes 1572880 | tf_op jit(solution)/shard_map/psum | solution.py:142
  366.9 2.1 multiply_reduce_fusion
  370.1 2.8 subtract_convert_fusion
  372.9 26.9 %reduce-scatter.2.cloned.1.call-done = bf16[3,64,128]{2,1,0:T(8,128)(2,1)} async-done(((bf16[3,512,128]{2,1,0:T(8,128)(2,1)}), bf16[3,64,128]{2,1,0:T(8,128)(2,1)}) %reduce-scatter.2.cloned.1.call-update) | async-done | bytes 49168 | tf_op jit(solution)/shard_map/reduce_scatter | solution.py:159
  (117 shorter events, 45.1 us)
Async XLA Ops:
  8.0 3.7 copy-start.16
  12.4 0.7 copy-start.9
  13.0 0.7 copy-start.7
  13.1 2.2 copy-start.19
  23.7 7.6 %copy-start.10 = (bf16[1536,128]{0,1:T(8,128)(2,1)S(1)}, bf16[1536,128]{0,1:T(8,128)(2,1)}, u32[]{:S(2)}) copy-start(bf16[1536,128]{0,1:T(8,128)(2,1)} %copy-done.9) | copy-start | bytes 1179652
  23.7 7.9 %copy-start.8 = (bf16[1536,128]{0,1:T(8,128)(2,1)S(1)}, bf16[1536,128]{0,1:T(8,128)(2,1)}, u32[]{:S(2)}) copy-start(bf16[1536,128]{0,1:T(8,128)(2,1)} %copy-done.7) | copy-start | bytes 1179652
  23.7 78.4 %all-to-all-start = ((bf16[8,6,128,256]{3,2,1,0:T(8,128)(2,1)}), bf16[8,6,128,256]{3,2,1,0:T(8,128)(2,1)}, u32[]{:S(2)}, u32[]{:S(2)}) async-start(bf16[8,6,128,256]{3,2,1,0:T(8,128)(2,1)} %broadcast_select_fusion.1), calls=%async_computation | async-start | bytes 6291456 | tf_op jit(solution)/shard_map/all_to_all | solution.py:52
  33.2 4.9 %copy-start.21 = (s32[12]{0:T(128)S(1)}, s32[12]{0:T(128)}, u32[]{:S(2)}) copy-start(s32[12]{0:T(128)} %param.11) | copy-start | bytes 148
  106.3 4.3 %copy-start.15 = (bf16[12,1,128,2,1,64]{2,5,1,3,0,4:T(8,128)(2,1)S(1)}, bf16[12,1,128,2,1,64]{2,5,1,3,0,4:T(8,128)(2,1)}, u32[]{:S(2)}) copy-start(bf16[12,1,128,2,1,64]{2,5,1,3,0,4:T(8,128)(2,1)} %copy.180) | copy-start | bytes 1179652
  112.4 8.4 %copy-start.2 = (bf16[12,4,128,2,2,64]{2,5,1,3,0,4:T(8,128)(2,1)}, bf16[12,4,128,2,2,64]{2,5,1,3,0,4:T(8,128)(2,1)S(1)}, u32[]{:S(2)}) copy-start(bf16[12,4,128,2,2,64]{2,5,1,3,0,4:T(8,128)(2,1)S(1)} %pad_maximum_fusion.1) | copy-start | bytes 9437188
  114.2 1.6 copy-start.17
  124.3 1.7 copy-start.4
  129.5 2.6 copy-start
  153.1 142.1 %all-to-all-start.1 = ((f32[8,6,128,256]{3,2,1,0:T(8,128)}), f32[8,6,128,256]{3,2,1,0:T(8,128)}, u32[]{:S(2)}, u32[]{:S(2)}) async-start(f32[8,6,128,256]{3,2,1,0:T(8,128)} %broadcast_select_fusion), calls=%async_computation.1 | async-start | bytes 12582912 | tf_op jit(solution)/shard_map/all_to_all | solution.py:114
  157.9 209.0 %all-reduce.3.cloned.1.call-start = ((), (), s32[]{:S(2)}) async-start(), calls=%async_computation.3 | async-start | bytes 3145728 | tf_op jit(solution)/shard_map/psum | solution.py:142
  158.1 2.4 copy-start.3
  165.9 4.2 %copy-start.13 = (bf16[12,128,2,64]{1,0,3,2:T(8,128)(2,1)S(1)}, bf16[12,128,2,64]{1,0,3,2:T(8,128)(2,1)}, u32[]{:S(2)}) copy-start(bf16[12,128,2,64]{1,0,3,2:T(8,128)(2,1)} %copy.203) | copy-start | bytes 1179652
  295.2 6.5 %copy-start.5 = (f32[2,8,128,256]{3,1,2,0:T(8,128)S(1)}, f32[2,8,128,256]{3,1,2,0:T(8,128)}, u32[]{:S(2)}) copy-start(f32[2,8,128,256]{3,1,2,0:T(8,128)} %copy.241) | copy-start | bytes 6291460
  315.8 6.1 %copy-start.11 = (bf16[1536,2,1,64]{0,3,2,1:T(8,128)(2,1)}, bf16[1536,2,1,64]{0,3,2,1:T(8,128)(2,1)S(1)}, u32[]{:S(2)}) copy-start(bf16[1536,2,1,64]{0,3,2,1:T(8,128)(2,1)S(1)} %copy.238) | copy-start | bytes 1179652
  321.9 2.9 copy-start.1
  324.8 75.0 %reduce-scatter.2.cloned.1.call-start = ((), (), s32[]{:S(2)}) async-start(), calls=%async_computation.4 | async-start | bytes 442368 | tf_op jit(solution)/shard_map/reduce_scatter | solution.py:159
  334.6 2.3 copy-start.12
  336.9 30.0 %copy-start.18 = (f32[512]{0:T(512)S(1)}, f32[512]{0:T(512)}, u32[]{:S(2)}) copy-start(f32[512]{0:T(512)} %param.7) | copy-start | bytes 6148
  366.9 2.1 copy-start.6
  369.0 1.1 copy-start.14
  369.0 1.1 copy-start.20
Sparse Core Ops, SparseCore 0:
  324.9 41.9 all-reduce.2
Sparse Core Ops, SparseCore 1:
  338.5 61.2 reduce-scatter.1
where the time goes:
time: 414 us; the launch traced here: 409 us
  waiting for transfers between devices  241 us (58%)
  local copies, waits for them, and re-layouts  77 us (19%)
  matrix products  31.7 us (8%)
  other arithmetic  30.4 us (7%)
  between operations  16.4 us (4%)
  starting transfers between devices  12.5 us (3%)
    all_to_all x1, waiting for transfers between devices, shards(): lax.all_to_all(returning, 'seq', split_axis=0, concat_axis=0, tiled=True)  122 us
    all_to_all x1, waiting for transfers between devices, shards(): lax.all_to_all(outgoing, 'seq', split_axis=0, concat_axis=0, tiled=True)  63.8 us
    psum x1, waiting for transfers between devices, shards(): lax.psum(grad_normed.astype(jnp.bfloat16), 'head').astype(jnp.float32)  28.4 us
    reduce_scatter x1, waiting for transfers between devices, shards(): lax.psum_scatter(terms.astype(jnp.bfloat16), 'seq', scatter_dimension=1,...  26.9 us
    unnamed x49, local copies, waits for them, and re-layouts  24 us
    gather x2, local copies, waits for them, and re-layouts, shards(): incoming.reshape(seq_count * capacity, BLOCK, kv_width)  8.53 us
    slice x2, local copies, waits for them, and re-layouts, shards(): remote = contrib[:, 1:].reshape(slot_count, BLOCK, kv_width)  8.51 us
  transfers between devices with their start and end apart: 4, of which 4 were waited for; matrix products, arithmetic and copies ran while one was open for 10% of the time, Pallas kernels for 0%

commit v1 on v0

v1 whole, which is shorter than its diff:
```python
import functools
import math

import jax
import jax.numpy as jnp
from jax import lax
from jax.experimental import pallas as pl
from jax.experimental.pallas import tpu as pltpu
from jax.sharding import PartitionSpec as P

HEAD_DIM = 64
BLOCK = 128
EXPD = 3
CHUNK = 256


EPS = 1e-06
F32 = jnp.float32
BF16 = jnp.bfloat16
VMEM_LIMIT = 50 * 1024 * 1024

CONTRACT_COLS = (((1,), (1,)), ((), ()))
CONTRACT_ROWS = (((0,), (0,)), ((), ()))


def rows_of(index, size):
    return pl.ds(pl.multiple_of(index * size, size), size)


def join_weights(w_ref, joined, cols):
    for member in range(3):
        joined[:, member * cols : (member + 1) * cols] = w_ref[member]


def project_kernel(sent_from, x_ref, gain_ref, w_ref, normed_ref, q_ref, kv_ref, out_ref, joined):
    cols = w_ref.shape[2]
    per_chunk = CHUNK // BLOCK
    join_weights(w_ref, joined, cols)

    def project(step, carry):
        rows = rows_of(step, CHUNK)
        x = x_ref[rows, :].astype(F32)
        inv_rms = lax.rsqrt(jnp.mean(x * x, axis=1, keepdims=True) + EPS)
        normed = (x * inv_rms * gain_ref[...]).astype(BF16)
        normed_ref[rows, :] = normed
        made = jnp.dot(normed, joined[...], preferred_element_type=F32).astype(BF16)
        q_ref[rows, :] = made[:, :cols]
        kv_ref[pl.ds(step * per_chunk, per_chunk)] = made[:, cols:].reshape(
            per_chunk, BLOCK, 2 * cols
        )
        return carry

    lax.fori_loop(0, x_ref.shape[0] // CHUNK, project, 0)

    def pack(slot, carry):
        out_ref[slot] = kv_ref[sent_from[slot]]
        return carry

    lax.fori_loop(0, out_ref.shape[0], pack, 0)


def attend_kernel(
    head, slots, counts, q_ref, kv_ref, slot_ref, x_ref, d_ref, layer_ref, gq_ref, own_ref, back_ref
):
    cols = q_ref.shape[1]
    heads_here = cols // HEAD_DIM
    scale = 1.0 / math.sqrt(HEAD_DIM)
    keys_all = (1 + EXPD) * BLOCK
    lane_head = lax.broadcasted_iota(jnp.int32, (BLOCK, cols), 1) // HEAD_DIM
    key_place = lax.broadcasted_iota(jnp.int32, (1, keys_all), 1)

    def spread(value):
        return jnp.concatenate(
            [jnp.where(lane_head == h, value, jnp.zeros_like(value)) for h in range(heads_here)],
            axis=0,
        )

    def merge(value):
        made = value[:BLOCK]
        for h in range(1, heads_here):
            made = jnp.where(lane_head == h, value[h * BLOCK : (h + 1) * BLOCK], made)
        return made

    def block_step(block, carry):
        rows = rows_of(block, BLOCK)
        places = [slots[block * EXPD + j] for j in range(EXPD)]
        own = kv_ref[block]
        listed = jnp.concatenate([own] + [slot_ref[place] for place in places], axis=0)
        keys = listed[:, :cols]
        values = listed[:, cols:]
        queries = spread(q_ref[rows, :])
        grads = spread(d_ref[rows, :])
        scores = lax.dot_general(queries, keys, CONTRACT_COLS, preferred_element_type=F32) * scale
        scores = jnp.where(key_place < (counts[block] + 1) * BLOCK, scores, -jnp.inf)
        powers = jnp.exp(scores - jnp.max(scores, axis=1, keepdims=True))
        attention = powers * (1.0 / jnp.sum(powers, axis=1, keepdims=True))
        low = attention.astype(BF16)
        attended = jnp.dot(low, values, preferred_element_type=F32)
        layer_ref[rows, :] = (x_ref[rows, :].astype(F32) + merge(attended)).astype(BF16)
        grad_attention = lax.dot_general(grads, values, CONTRACT_COLS, preferred_element_type=F32)
        row_dot = jnp.sum(grads.astype(F32) * attended, axis=1, keepdims=True)
        grad_scores = (attention * (grad_attention - row_dot) * scale).astype(BF16)
        gq_ref[rows, :] = merge(jnp.dot(grad_scores, keys, preferred_element_type=F32)).astype(BF16)
        grad_keys = lax.dot_general(grad_scores, queries, CONTRACT_ROWS, preferred_element_type=F32)
        grad_values = lax.dot_general(low, grads, CONTRACT_ROWS, preferred_element_type=F32)
        own_ref[block] = jnp.concatenate([grad_keys[:BLOCK], grad_values[:BLOCK]], axis=1)
        for j, place in enumerate(places):
            part = slice((j + 1) * BLOCK, (j + 2) * BLOCK)
            back_ref[place] = jnp.concatenate([grad_keys[part], grad_values[part]], axis=1).astype(
                BF16
            )
        return carry

    lax.fori_loop(0, kv_ref.shape[0], block_step, 0)


def weight_kernel(
    sent_from,
    filled,
    own_ref,
    back_ref,
    gq_ref,
    normed_ref,
    x_ref,
    gain_ref,
    w_ref,
    gn_ref,
    term_ref,
    gw_ref,
    joined,
    total,
    sums,
    *,
    node_count,
):
    cols = w_ref.shape[2]
    width = w_ref.shape[1]
    row_count = x_ref.shape[0]
    per_chunk = CHUNK // BLOCK
    join_weights(w_ref, joined, cols)
    total[...] = own_ref[...]
    sums[...] = jnp.zeros_like(sums)

    def gather(slot, carry):
        @pl.when(filled[slot] > 0)
        def _():
            place = sent_from[slot]
            total[place] = total[place] + back_ref[slot].astype(F32)

        return carry

    lax.fori_loop(0, back_ref.shape[0], gather, 0)

    def chunk_step(step, carry):
        rows = rows_of(step, CHUNK)
        grad_kv = total[pl.ds(step * per_chunk, per_chunk)].reshape(CHUNK, 2 * cols).astype(BF16)
        grads = jnp.concatenate([gq_ref[rows, :], grad_kv], axis=1)
        grad_normed = lax.dot_general(grads, joined[...], CONTRACT_COLS, preferred_element_type=F32)
        for part in range(width // cols):
            gn_ref[part, rows, :] = grad_normed[:, part * cols : (part + 1) * cols].astype(BF16)
        term = jnp.sum(
            x_ref[rows, :].astype(F32) * gain_ref[...] * grad_normed, axis=1, keepdims=True
        )
        for inner in range(per_chunk):
            piece = jnp.broadcast_to(term[inner * BLOCK : (inner + 1) * BLOCK], (BLOCK, BLOCK))
            term_ref[step * per_chunk + inner] = piece.T[:8]
        sums[...] += lax.dot_general(
            normed_ref[rows, :], grads, CONTRACT_ROWS, preferred_element_type=F32
        )
        return carry

    lax.fori_loop(0, row_count // CHUNK, chunk_step, 0)
    seq_count = gw_ref.shape[0]
    share = width // seq_count
    factor = 1.0 / math.sqrt(node_count)
    for peer in range(seq_count):
        for member in range(3):
            gw_ref[peer, member] = (
                sums[peer * share : (peer + 1) * share, member * cols : (member + 1) * cols]
                * factor
            ).astype(BF16)


def input_kernel(head, gn_ref, term_ref, x_ref, mine_ref, d_ref, gain_ref, out_ref):
    width = x_ref.shape[1]

    def block_step(block, carry):
        rows = rows_of(block, BLOCK)
        x = x_ref[rows, :].astype(F32)
        inv_rms = lax.rsqrt(jnp.mean(x * x, axis=1, keepdims=True) + EPS)
        grad = gn_ref[0, rows, :].astype(F32)
        for part in range(1, gn_ref.shape[0]):
            grad = grad + gn_ref[part, rows, :].astype(F32)
        row = term_ref[pl.ds(block, 1), :]
        term = jnp.broadcast_to(row, (BLOCK, BLOCK)).T[:, :1] * (1.0 / width)
        cubed = inv_rms * inv_rms * inv_rms
        out_ref[rows, :] = (
            d_ref[rows, :].astype(F32)
            + inv_rms * gain_ref[...] * grad
            - mine_ref[rows, :].astype(F32) * (cubed * term)
        ).astype(BF16)
        return carry

    lax.fori_loop(0, x_ref.shape[0] // BLOCK, block_step, 0)


def whole(shape):
    return pl.BlockSpec(shape, lambda i, *refs: (0,) * len(shape))


def run(kernel, scalars, args, outs, scratch=(), columns=(), col_count=128):
    if columns and col_count % 128:
        args = [
            lax.dynamic_slice_in_dim(value, scalars[0][0] * col_count, col_count, 1)
            if place in columns
            else value
            for place, value in enumerate(args)
        ]
        columns = ()

    def spec(place, value):
        if place in columns:
            return pl.BlockSpec(
                (value.shape[0], col_count), lambda i, head, *refs: (0, head[0])
            )
        return whole(value.shape)

    return pl.pallas_call(
        kernel,
        out_shape=outs,
        grid_spec=pltpu.PrefetchScalarGridSpec(
            num_scalar_prefetch=len(scalars),
            grid=(1,),
            in_specs=[spec(place, value) for place, value in enumerate(args)],
            out_specs=jax.tree.map(lambda out: whole(out.shape), outs),
            scratch_shapes=list(scratch),
        ),
        compiler_params=pltpu.CompilerParams(vmem_limit_bytes=VMEM_LIMIT),
    )(*scalars, *args)


def shards(node_features, gain, w_qkv, d_out, pattern, counts):
    seq_count = lax.axis_size("seq")
    my_index = lax.axis_index("seq")
    row_count, width = node_features.shape
    block_count = row_count // BLOCK
    col_count = w_qkv.shape[2]
    head_count = width // col_count
    slot_count = block_count * EXPD
    capacity = max(2, 3 * slot_count // (2 * seq_count))
    slots_all = seq_count * capacity
    kv_width = 2 * col_count
    head = lax.axis_index("head").astype(jnp.int32).reshape(1)
    gain_row = gain.reshape(1, width)
    shape = jax.ShapeDtypeStruct

    owners = (pattern // block_count).reshape(seq_count, slot_count)
    in_owner = (pattern % block_count).reshape(seq_count, slot_count)
    before = jnp.arange(slot_count)[:, None] > jnp.arange(slot_count)[None, :]
    same = owners[:, :, None] == owners[:, None, :]
    ranks = jnp.sum((same & before[None]).astype(jnp.int32), axis=2)
    places = jnp.arange(capacity, dtype=jnp.int32)
    picked = (owners[:, None, :] == my_index) & (ranks[:, None, :] == places[None, :, None])
    sent_from = jnp.sum(jnp.where(picked, in_owner[:, None, :], 0), axis=2).reshape(-1)
    filled = jnp.any(picked, axis=2).astype(jnp.int32).reshape(-1)
    my_slots = lax.dynamic_index_in_dim(owners * capacity + ranks, my_index, 0, keepdims=False)

    normed, queries, kv_local, outgoing = run(
        project_kernel,
        (sent_from,),
        (node_features, gain_row, w_qkv),
        (
            shape((row_count, width), BF16),
            shape((row_count, col_count), BF16),
            shape((block_count, BLOCK, kv_width), BF16),
            shape((slots_all, BLOCK, kv_width), BF16),
        ),
        scratch=(pltpu.VMEM((width, 3 * col_count), BF16),),
    )
    incoming = lax.all_to_all(outgoing, "seq", split_axis=0, concat_axis=0, tiled=True)
    layer_output, grad_queries, own, returning = run(
        attend_kernel,
        (head, my_slots, counts),
        (queries, kv_local, incoming, node_features, d_out),
        (
            shape((row_count, col_count), BF16),
            shape((row_count, col_count), BF16),
            shape((block_count, BLOCK, kv_width), F32),
            shape((slots_all, BLOCK, kv_width), BF16),
        ),
        columns=(3, 4),
        col_count=col_count,
    )
    returned = lax.all_to_all(returning, "seq", split_axis=0, concat_axis=0, tiled=True)
    share = width // seq_count
    grad_parts, terms, weight_parts = run(
        functools.partial(weight_kernel, node_count=row_count * seq_count),
        (sent_from, filled),
        (own, returned, grad_queries, normed, node_features, gain_row, w_qkv),
        (
            shape((head_count, row_count, col_count), BF16),
            shape((block_count, 8, BLOCK), F32),
            shape((seq_count, 3, share, col_count), BF16),
        ),
        scratch=(
            pltpu.VMEM((width, 3 * col_count), BF16),
            pltpu.VMEM((block_count, BLOCK, kv_width), F32),
            pltpu.VMEM((width, 3 * col_count), F32),
        ),
    )
    row_terms = lax.psum(terms[:, 0, :], "head")
    grad_parts = lax.all_to_all(grad_parts, "head", split_axis=0, concat_axis=0, tiled=True)
    weight_parts = lax.all_to_all(weight_parts, "seq", split_axis=0, concat_axis=0, tiled=True)
    gain_mine = lax.dynamic_slice_in_dim(gain_row, head[0] * col_count, col_count, 1)
    grad_input = run(
        input_kernel,
        (head,),
        (grad_parts, row_terms, node_features, node_features, d_out, gain_mine),
        shape((row_count, col_count), BF16),
        columns=(3, 4),
        col_count=col_count,
    )
    grad_weights = jnp.sum(weight_parts.astype(F32), axis=0)
    return (layer_output, grad_input, grad_weights)


def solution(mesh):
    in_specs = (P("seq", None), P(), P(None, None, "head"), P("seq", None), P(), P("seq"))
    out_specs = (P("seq", "head"), P("seq", "head"), P(None, "seq", "head"))
    return jax.shard_map(shards, mesh=mesh, in_specs=in_specs, out_specs=out_specs, check_vma=False)
```

time: 414 us -> 240 us (0.58); the launches traced: 409 us -> 240 us
  waiting for transfers between devices: 241 us -> 141 us
  local copies, waits for them, and re-layouts: 77 us -> 6.18 us
  blocking collectives: 0 us -> 37.3 us
  Pallas kernels: 0 us -> 35.5 us
  matrix products: 31.7 us -> 0 us
  other arithmetic: 30.4 us -> 3.54 us
  between operations: 16.4 us -> 0.74 us
    all_to_all x1, waiting for transfers between devices: 122 us -> 69.8 us  [shards(): lax.all_to_all(returning, 'seq', split_axis=0, concat_axis=0, tiled=True)]
    pallas_call x0 -> x4, Pallas kernels: none -> 35.5 us  [run(): pl.pallas_call(kernel, out_shape=outs, grid_spec=pltpu.PrefetchScalarGrid...]
    dot_general x16 -> x0, matrix products: 31.7 us -> none  [the longest x1 3.47 us: shards(): jnp.einsum('bqhe,btkhe->bhqtk', grad_blocks, value_side, preferred_elemen...]
    psum x1 -> x0, waiting for transfers between devices: 28.4 us -> none  [shards(): lax.psum(grad_normed.astype(jnp.bfloat16), 'head').astype(jnp.float32)]
    reduce_scatter x1 -> x0, waiting for transfers between devices: 26.9 us -> none  [shards(): lax.psum_scatter(terms.astype(jnp.bfloat16), 'seq', scatter_dimension=1,...]
    psum x0 -> x1, blocking collectives: none -> 21.5 us  [shards(): row_terms = lax.psum(terms[:, 0, :], 'head')]
    unnamed x49 -> x18, local copies, waits for them, and re-layouts: 24 us -> 5.22 us
    gather x4 -> x0, local copies, waits for them, and re-layouts: 17 us -> none  [the longest x2 8.53 us: shards(): incoming.reshape(seq_count * capacity, BLOCK, kv_width)]
  transfers between devices with their start and end apart: 4 -> 3, of which waited for: 4 -> 2; matrix products, arithmetic and copies ran while one was open for 10% -> 1% of each run, Pallas kernels for 0% -> 0%
where the time goes in v1:
time: 240 us
  waiting for transfers between devices  141 us (59%)
  blocking collectives  37.3 us (16%)
  Pallas kernels  35.5 us (15%)
  starting transfers between devices  15.7 us (7%)
  local copies, waits for them, and re-layouts  6.18 us (3%)
  other arithmetic  3.54 us (1%)
    all_to_all x1, waiting for transfers between devices, shards(): lax.all_to_all(outgoing, 'seq', split_axis=0, concat_axis=0, tiled=True)  70.8 us
    all_to_all x1, waiting for transfers between devices, shards(): lax.all_to_all(returning, 'seq', split_axis=0, concat_axis=0, tiled=True)  69.8 us
    pallas_call x4, Pallas kernels, run(): pl.pallas_call(kernel, out_shape=outs, grid_spec=pltpu.PrefetchScalarGrid...  35.5 us
    psum x1, blocking collectives, shards(): row_terms = lax.psum(terms[:, 0, :], 'head')  21.5 us
    all_to_all x1, blocking collectives, shards(): lax.all_to_all(weight_parts, 'seq', split_axis=0, concat_axis=0, tiled=True)  15.8 us
    all_to_all x1, starting transfers between devices, shards(): lax.all_to_all(outgoing, 'seq', split_axis=0, concat_axis=0, tiled=True)  7.41 us
    unnamed x18, local copies, waits for them, and re-layouts  5.22 us
  transfers between devices with their start and end apart: 3, of which 2 were waited for; matrix products, arithmetic and copies ran while one was open for 1% of the time, Pallas kernels for 0%

profile of v1, /device:TPU:0, one launch (start us, length us, event | category | flops | bytes accessed | tf_op | source)
XLA Modules:
  0.0 239.5 jit_solution(7287509609395184954)
XLA Ops:
  0.7 0.7 add_select_fusion
  1.4 0.1 copy.33
  1.5 0.1 broadcast_in_dim.19
  1.5 0.1 copy.29
  1.6 0.1 reshape.47
  1.7 0.1 copy.30
  1.8 0.8 convert_reduce_fusion.1
  2.6 0.1 copy.31
  2.7 0.2 select_reduce_fusion
  2.8 0.1 copy.34
  2.9 0.1 reshape.48.sent_from
  3.0 1.0 copy-done.1
  4.0 0.7 copy-done.6
  4.7 6.4 %shard_map.85 = (bf16[1536,512]{1,0:T(8,128)(2,1)S(1)}, bf16[1536,128]{1,0:T(8,128)(2,1)S(1)}, bf16[12,128,256]{2,1,0:T(8,128)(2,1)S(1)}, bf16[48,128,256]{2,1,0:T(8,128)(2,1)}) custom-call(s32[48]{0:T(128)S(1)} %reshape.48.sent_from, bf16[1536,512]{1,0:T(8,128)(2,1)} %mine_ref.1, f32[1,512]{1,0:T(1,128)S(1)} %bitcast.8, bf16[3,512,128]{2,1,0:T(8,128)(2,1)S(1)} %copy-done.1), custom_call_target="tpu_custom_call" | custom-call | tf_op jit(solution)/shard_map/pallas_call | solution.py:228
  11.1 1.1 copy-done.3
  12.2 7.4 %all-to-all-start = ((bf16[48,128,256]{2,1,0:T(8,128)(2,1)}), bf16[48,128,256]{2,1,0:T(8,128)(2,1)}, u32[]{:S(2)}, u32[]{:S(2)}) async-start(bf16[48,128,256]{2,1,0:T(8,128)(2,1)} %get-tuple-element.16), calls=%async_computation | async-start | bytes 6291456 | tf_op jit(solution)/shard_map/all_to_all | solution.py:280
  19.6 70.8 %all-to-all-done.slot_ref = bf16[48,128,256]{2,1,0:T(8,128)(2,1)} async-done(((bf16[48,128,256]{2,1,0:T(8,128)(2,1)}), bf16[48,128,256]{2,1,0:T(8,128)(2,1)}, u32[]{:S(2)}, u32[]{:S(2)}) %all-to-all-start) | async-done | bytes 3145760 | tf_op jit(solution)/shard_map/all_to_all | solution.py:280
  90.4 16.4 %shard_map.86 = (bf16[1536,128]{1,0:T(8,128)(2,1)}, bf16[1536,128]{1,0:T(8,128)(2,1)S(1)}, f32[12,128,256]{2,1,0:T(8,128)S(1)}, bf16[48,128,256]{2,1,0:T(8,128)(2,1)}) custom-call(s32[1]{0:T(128)} %bitcast.head, s32[36]{0:T(128)S(1)} %dynamic-slice_bitcast_fusion.1.slots, s32[12]{0:T(128)S(1)} %copy-done.8, bf16[1536,128]{1,0:T(8,128)(2,1)S(1)} %get-tuple-element.14.q_ref, ...), custom_call_target="tpu_custom_call" | custom-call | tf_op jit(solution)/shard_map/pallas_call | solution.py:228
  106.9 1.2 copy-done.4
  108.1 4.6 %all-to-all-start.1 = ((bf16[48,128,256]{2,1,0:T(8,128)(2,1)}), bf16[48,128,256]{2,1,0:T(8,128)(2,1)}, u32[]{:S(2)}, u32[]{:S(2)}) async-start(bf16[48,128,256]{2,1,0:T(8,128)(2,1)} %get-tuple-element.19), calls=%async_computation.1 | async-start | bytes 6291456 | tf_op jit(solution)/shard_map/all_to_all | solution.py:294
  112.7 0.2 fusion.1
  112.9 0.1 copy.35
  112.9 0.1 reshape.50.filled
  113.0 69.8 %all-to-all-done.1.back_ref = bf16[48,128,256]{2,1,0:T(8,128)(2,1)} async-done(((bf16[48,128,256]{2,1,0:T(8,128)(2,1)}), bf16[48,128,256]{2,1,0:T(8,128)(2,1)}, u32[]{:S(2)}, u32[]{:S(2)}) %all-to-all-start.1) | async-done | bytes 3145760 | tf_op jit(solution)/shard_map/all_to_all | solution.py:294
  182.9 8.0 %shard_map.87 = (bf16[4,1536,128]{2,1,0:T(8,128)(2,1)S(1)}, f32[12,8,128]{2,1,0:T(8,128)S(1)}, bf16[8,3,64,128]{3,2,1,0:T(8,128)(2,1)S(1)}) custom-call(s32[48]{0:T(128)S(1)} %reshape.48.sent_from, s32[48]{0:T(128)S(1)} %reshape.50.filled, f32[12,128,256]{2,1,0:T(8,128)} %copy-done.4, bf16[48,128,256]{2,1,0:T(8,128)(2,1)} %all-to-all-done.1.back_ref, ...), custom_call_target="tpu_custom_call" | custom-call | tf_op jit(solution)/shard_map/pallas_call | solution.py:228
  190.8 1.2 copy-done.5
  192.0 15.8 %all_to_all.20 = bf16[8,3,64,128]{3,2,1,0:T(8,128)(2,1)} all-to-all(bf16[8,3,64,128]{3,2,1,0:T(8,128)(2,1)S(1)} %get-tuple-element.24), channel_id=1, replica_groups=mesh['seq'=8,'head'=4] {'seq'}, dimensions={0} | all-to-all | bytes 786432 | tf_op jit(solution)/shard_map/all_to_all | solution.py:313
  207.8 3.7 %all-to-all-start.2 = ((bf16[4,1536,128]{2,1,0:T(8,128)(2,1)}), bf16[4,1536,128]{2,1,0:T(8,128)(2,1)S(1)}, u32[]{:S(2)}, u32[]{:S(2)}) async-start(bf16[4,1536,128]{2,1,0:T(8,128)(2,1)} %copy-done.5), calls=%async_computation.2 | async-start | bytes 3145728 | tf_op jit(solution)/shard_map/all_to_all | solution.py:312
  211.5 0.1 dynamic-slice_bitcast_fusion.gain_ref
  211.6 21.5 %psum.7.term_ref = f32[12,128]{1,0:T(8,128)S(1)} all-reduce(f32[12,128]{1,0:T(8,128)S(1)} %slice_bitcast_fusion), channel_id=1, replica_groups=mesh['seq'=8,'head'=4] {'head'}, use_global_device_ids=true, to_apply=%region_3.4 | all-reduce | flops 1536 | bytes 12288 | tf_op jit(solution)/shard_map/psum | solution.py:311
  233.1 1.7 convert_reduce_fusion
  234.8 4.7 %shard_map.88 = bf16[1536,128]{1,0:T(8,128)(2,1)} custom-call(s32[1]{0:T(128)} %bitcast.head, bf16[4,1536,128]{2,1,0:T(8,128)(2,1)S(1)} %all-to-all-done.2.gn_ref, f32[12,128]{1,0:T(8,128)S(1)} %psum.7.term_ref, bf16[1536,512]{1,0:T(8,128)(2,1)S(1)} %copy-done, bf16[1536,512]{1,0:T(8,128)(2,1)S(1)} %copy-done, bf16[1536,512]{1,0:T(8,128)(2,1)} %d_ref.3, ...), custom_call_target="tpu_custom_call" | custom-call | tf_op jit(solution)/shard_map/pallas_call | solution.py:228
  (21 shorter events, 0.1 us)
Async XLA Ops:
  3.0 1.0 copy-start.1
  4.0 0.7 copy-start.6
  11.1 1.1 copy-start.3
  12.2 78.2 %copy-start.8 = (s32[12]{0:T(128)S(1)}, s32[12]{0:T(128)}, u32[]{:S(2)}) copy-start(s32[12]{0:T(128)} %counts.1) | copy-start | bytes 148
  12.2 78.2 %all-to-all-start = ((bf16[48,128,256]{2,1,0:T(8,128)(2,1)}), bf16[48,128,256]{2,1,0:T(8,128)(2,1)}, u32[]{:S(2)}, u32[]{:S(2)}) async-start(bf16[48,128,256]{2,1,0:T(8,128)(2,1)} %get-tuple-element.16), calls=%async_computation | async-start | bytes 6291456 | tf_op jit(solution)/shard_map/all_to_all | solution.py:280
  106.8 1.2 copy-start.4
  108.1 74.8 %copy-start.2 = (bf16[3,512,128]{2,1,0:T(8,128)(2,1)S(1)}, bf16[3,512,128]{2,1,0:T(8,128)(2,1)}, u32[]{:S(2)}) copy-start(bf16[3,512,128]{2,1,0:T(8,128)(2,1)} %w_ref.3) | copy-start | bytes 1179652
  108.1 74.8 %copy-start.7 = (f32[512]{0:T(512)S(1)}, f32[512]{0:T(512)}, u32[]{:S(2)}) copy-start(f32[512]{0:T(512)} %param.7) | copy-start | bytes 6148
  108.1 74.8 %all-to-all-start.1 = ((bf16[48,128,256]{2,1,0:T(8,128)(2,1)}), bf16[48,128,256]{2,1,0:T(8,128)(2,1)}, u32[]{:S(2)}, u32[]{:S(2)}) async-start(bf16[48,128,256]{2,1,0:T(8,128)(2,1)} %get-tuple-element.19), calls=%async_computation.1 | async-start | bytes 6291456 | tf_op jit(solution)/shard_map/all_to_all | solution.py:294
  190.8 1.2 copy-start.5
  207.8 27.0 %copy-start = (bf16[1536,512]{1,0:T(8,128)(2,1)S(1)}, bf16[1536,512]{1,0:T(8,128)(2,1)}, u32[]{:S(2)}) copy-start(bf16[1536,512]{1,0:T(8,128)(2,1)} %mine_ref.1) | copy-start | bytes 4718596
  207.8 27.0 %all-to-all-start.2 = ((bf16[4,1536,128]{2,1,0:T(8,128)(2,1)}), bf16[4,1536,128]{2,1,0:T(8,128)(2,1)S(1)}, u32[]{:S(2)}, u32[]{:S(2)}) async-start(bf16[4,1536,128]{2,1,0:T(8,128)(2,1)} %copy-done.5), calls=%async_computation.2 | async-start | bytes 3145728 | tf_op jit(solution)/shard_map/all_to_all | solution.py:312

commit v2 on v1

--- a/solution.py
+++ b/solution.py
@@ -60,7 +60,7 @@
 
 
 def attend_kernel(
-    head, slots, counts, q_ref, kv_ref, slot_ref, x_ref, d_ref, layer_ref, gq_ref, own_ref, back_ref
+    slots, counts, q_ref, kv_ref, slot_ref, x_ref, d_ref, layer_ref, gq_ref, own_ref, back_ref
 ):
     cols = q_ref.shape[1]
     heads_here = cols // HEAD_DIM
@@ -114,32 +114,14 @@
     lax.fori_loop(0, kv_ref.shape[0], block_step, 0)
 
 
-def weight_kernel(
-    sent_from,
-    filled,
-    own_ref,
-    back_ref,
-    gq_ref,
-    normed_ref,
-    x_ref,
-    gain_ref,
-    w_ref,
-    gn_ref,
-    term_ref,
-    gw_ref,
-    joined,
-    total,
-    sums,
-    *,
-    node_count,
+def gather_kernel(
+    sent_from, filled, own_ref, back_ref, gq_ref, normed_ref, grads_ref, gw_ref, total, sums, *, node_count
 ):
-    cols = w_ref.shape[2]
-    width = w_ref.shape[1]
-    row_count = x_ref.shape[0]
+    cols = gq_ref.shape[1]
+    width = normed_ref.shape[1]
     per_chunk = CHUNK // BLOCK
-    join_weights(w_ref, joined, cols)
+    sums[...] = jnp.zeros_like(sums)
     total[...] = own_ref[...]
-    sums[...] = jnp.zeros_like(sums)
 
     def gather(slot, carry):
         @pl.when(filled[slot] > 0)
@@ -155,21 +137,13 @@
         rows = rows_of(step, CHUNK)
         grad_kv = total[pl.ds(step * per_chunk, per_chunk)].reshape(CHUNK, 2 * cols).astype(BF16)
         grads = jnp.concatenate([gq_ref[rows, :], grad_kv], axis=1)
-        grad_normed = lax.dot_general(grads, joined[...], CONTRACT_COLS, preferred_element_type=F32)
-        for part in range(width // cols):
-            gn_ref[part, rows, :] = grad_normed[:, part * cols : (part + 1) * cols].astype(BF16)
-        term = jnp.sum(
-            x_ref[rows, :].astype(F32) * gain_ref[...] * grad_normed, axis=1, keepdims=True
-        )
-        for inner in range(per_chunk):
-            piece = jnp.broadcast_to(term[inner * BLOCK : (inner + 1) * BLOCK], (BLOCK, BLOCK))
-            term_ref[step * per_chunk + inner] = piece.T[:8]
+        grads_ref[rows, :] = grads
         sums[...] += lax.dot_general(
             normed_ref[rows, :], grads, CONTRACT_ROWS, preferred_element_type=F32
         )
         return carry
 
-    lax.fori_loop(0, row_count // CHUNK, chunk_step, 0)
+    lax.fori_loop(0, gq_ref.shape[0] // CHUNK, chunk_step, 0)
     seq_count = gw_ref.shape[0]
     share = width // seq_count
     factor = 1.0 / math.sqrt(node_count)
@@ -181,61 +155,164 @@
             ).astype(BF16)
 
 
-def input_kernel(head, gn_ref, term_ref, x_ref, mine_ref, d_ref, gain_ref, out_ref):
-    width = x_ref.shape[1]
-
-    def block_step(block, carry):
-        rows = rows_of(block, BLOCK)
+def exchange_kernel(
+    grads_ref,
+    gw_ref,
+    x_ref,
+    mine_ref,
+    d_ref,
+    gain_ref,
+    gain_mine_ref,
+    w_ref,
+    out_ref,
+    weights_ref,
+    joined,
+    parts,
+    arrived,
+    terms,
+    terms_in,
+    gw_in,
+    part_send,
+    part_recv,
+    term_send,
+    term_recv,
+    gw_send,
+    gw_recv,
+):
+    cols = w_ref.shape[2]
+    row_count, width = x_ref.shape
+    head_count = parts.shape[0]
+    seq_count = gw_ref.shape[0]
+    per_chunk = CHUNK // BLOCK
+    chunks = row_count // CHUNK
+    head = lax.axis_index("head")
+    seq = lax.axis_index("seq")
+    mesh_type = pl.DeviceIdType.MESH
+
+    def head_peer(k):
+        return lax.rem(head + k, head_count)
+
+    def seq_peer(k):
+        return lax.rem(seq + k, seq_count)
+
+    barrier = pltpu.get_barrier_semaphore()
+    for k in range(1, head_count):
+        pl.semaphore_signal(
+            barrier, inc=1, device_id={"head": head_peer(k)}, device_id_type=mesh_type
+        )
+    for k in range(1, seq_count):
+        pl.semaphore_signal(
+            barrier, inc=1, device_id={"seq": seq_peer(k)}, device_id_type=mesh_type
+        )
+    pl.semaphore_wait(barrier, head_count + seq_count - 2)
+
+    def weight_copy(k):
+        return pltpu.make_async_remote_copy(
+            src_ref=gw_ref.at[seq_peer(k)],
+            dst_ref=gw_in.at[k - 1],
+            send_sem=gw_send.at[k - 1],
+            recv_sem=gw_recv.at[k - 1],
+            device_id={"seq": seq_peer(k)},
+            device_id_type=mesh_type,
+        )
+
+    def part_copy(k, step):
+        rows = rows_of(step, CHUNK)
+        return pltpu.make_async_remote_copy(
+            src_ref=parts.at[head_peer(k), rows],
+            dst_ref=arrived.at[k - 1, rows],
+            send_sem=part_send.at[k - 1, step],
+            recv_sem=part_recv.at[k - 1, step],
+            device_id={"head": head_peer(k)},
+            device_id_type=mesh_type,
+        )
+
+    def term_copy(k):
+        return pltpu.make_async_remote_copy(
+            src_ref=terms,
+            dst_ref=terms_in.at[k - 1],
+            send_sem=term_send.at[k - 1],
+            recv_sem=term_recv.at[k - 1],
+            device_id={"head": head_peer(k)},
+            device_id_type=mesh_type,
+        )
+
+    for k in range(1, seq_count):
+        weight_copy(k).start()
+    join_weights(w_ref, joined, cols)
+
+    def chunk_step(step, carry):
+        rows = rows_of(step, CHUNK)
+        grad_normed = lax.dot_general(
+            grads_ref[rows, :], joined[...], CONTRACT_COLS, preferred_element_type=F32
+        )
+        for part in range(head_count):
+            parts[part, rows, :] = grad_normed[:, part * cols : (part + 1) * cols].astype(BF16)
+        for k in range(1, head_count):
+            part_copy(k, step).start()
+        term = jnp.sum(
+            x_ref[rows, :].astype(F32) * gain_ref[...] * grad_normed, axis=1, keepdims=True
+        )
+        for inner in range(per_chunk):
+            piece = jnp.broadcast_to(term[inner * BLOCK : (inner + 1) * BLOCK], (BLOCK, BLOCK))
+            terms[step * per_chunk + inner] = piece.T[:8]
+        return carry
+
+    lax.fori_loop(0, chunks, chunk_step, 0)
+    for k in range(1, head_count):
+        term_copy(k).start()
+    for k in range(1, seq_count):
+        weight_copy(k).wait()
+    total = gw_ref[seq].astype(F32)
+    for k in range(1, seq_count):
+        total = total + gw_in[k - 1].astype(F32)
+    weights_ref[...] = total
+    for k in range(1, head_count):
+        term_copy(k).wait()
+
+    def final_step(step, carry):
+        rows = rows_of(step, CHUNK)
         x = x_ref[rows, :].astype(F32)
         inv_rms = lax.rsqrt(jnp.mean(x * x, axis=1, keepdims=True) + EPS)
-        grad = gn_ref[0, rows, :].astype(F32)
-        for part in range(1, gn_ref.shape[0]):
-            grad = grad + gn_ref[part, rows, :].astype(F32)
-        row = term_ref[pl.ds(block, 1), :]
-        term = jnp.broadcast_to(row, (BLOCK, BLOCK)).T[:, :1] * (1.0 / width)
+        columns = []
+        for inner in range(per_chunk):
+            row = terms[step * per_chunk + inner]
+            for k in range(1, head_count):
+                row = row + terms_in[k - 1, step * per_chunk + inner]
+            columns.append(jnp.broadcast_to(row[:1], (BLOCK, BLOCK)).T[:, :1])
+        term = jnp.concatenate(columns, axis=0) * (1.0 / width)
+        for k in range(1, head_count):
+            part_copy(k, step).wait()
+        grad = parts[head, rows, :].astype(F32)
+        for k in range(1, head_count):
+            grad = grad + arrived[k - 1, rows, :].astype(F32)
         cubed = inv_rms * inv_rms * inv_rms
         out_ref[rows, :] = (
             d_ref[rows, :].astype(F32)
-            + inv_rms * gain_ref[...] * grad
+            + inv_rms * gain_mine_ref[...] * grad
             - mine_ref[rows, :].astype(F32) * (cubed * term)
         ).astype(BF16)
         return carry
 
-    lax.fori_loop(0, x_ref.shape[0] // BLOCK, block_step, 0)
+    lax.fori_loop(0, chunks, final_step, 0)
 
 
 def whole(shape):
     return pl.BlockSpec(shape, lambda i, *refs: (0,) * len(shape))
 
 
-def run(kernel, scalars, args, outs, scratch=(), columns=(), col_count=128):
-    if columns and col_count % 128:
-        args = [
-            lax.dynamic_slice_in_dim(value, scalars[0][0] * col_count, col_count, 1)
-            if place in columns
-            else value
-            for place, value in enumerate(args)
-        ]
-        columns = ()
-
-    def spec(place, value):
-        if place in columns:
-            return pl.BlockSpec(
-                (value.shape[0], col_count), lambda i, head, *refs: (0, head[0])
-            )
-        return whole(value.shape)
-
+def run(kernel, scalars, args, outs, scratch=(), **params):
     return pl.pallas_call(
         kernel,
         out_shape=outs,
         grid_spec=pltpu.PrefetchScalarGridSpec(
             num_scalar_prefetch=len(scalars),
             grid=(1,),
-            in_specs=[spec(place, value) for place, value in enumerate(args)],
+            in_specs=[whole(value.shape) for value in args],
             out_specs=jax.tree.map(lambda out: whole(out.shape), outs),
             scratch_shapes=list(scratch),
         ),
-        compiler_params=pltpu.CompilerParams(vmem_limit_bytes=VMEM_LIMIT),
+        compiler_params=pltpu.CompilerParams(vmem_limit_bytes=VMEM_LIMIT, **params),
     )(*scalars, *args)
 
 
@@ -250,8 +327,12 @@
     capacity = max(2, 3 * slot_count // (2 * seq_count))
     slots_all = seq_count * capacity
     kv_width = 2 * col_count
-    head = lax.axis_index("head").astype(jnp.int32).reshape(1)
+    col_start = lax.axis_index("head") * col_count
     gain_row = gain.reshape(1, width)
+    x_mine, d_mine, gain_mine = (
+        lax.dynamic_slice_in_dim(value, col_start, col_count, 1)
+        for value in (node_features, d_out, gain_row)
+    )
     shape = jax.ShapeDtypeStruct
 
     owners = (pattern // block_count).reshape(seq_count, slot_count)
@@ -280,47 +361,58 @@
     incoming = lax.all_to_all(outgoing, "seq", split_axis=0, concat_axis=0, tiled=True)
     layer_output, grad_queries, own, returning = run(
         attend_kernel,
-        (head, my_slots, counts),
-        (queries, kv_local, incoming, node_features, d_out),
+        (my_slots, counts),
+        (queries, kv_local, incoming, x_mine, d_mine),
         (
             shape((row_count, col_count), BF16),
             shape((row_count, col_count), BF16),
             shape((block_count, BLOCK, kv_width), F32),
             shape((slots_all, BLOCK, kv_width), BF16),
         ),
-        columns=(3, 4),
-        col_count=col_count,
     )
     returned = lax.all_to_all(returning, "seq", split_axis=0, concat_axis=0, tiled=True)
     share = width // seq_count
-    grad_parts, terms, weight_parts = run(
-        functools.partial(weight_kernel, node_count=row_count * seq_count),
+    grads, weight_parts = run(
+        functools.partial(gather_kernel, node_count=row_count * seq_count),
         (sent_from, filled),
-        (own, returned, grad_queries, normed, node_features, gain_row, w_qkv),
+        (own, returned, grad_queries, normed),
         (
-            shape((head_count, row_count, col_count), BF16),
-            shape((block_count, 8, BLOCK), F32),
+            shape((row_count, 3 * col_count), BF16),
             shape((seq_count, 3, share, col_count), BF16),
+        ),
+        scratch=(
+            pltpu.VMEM((block_count, BLOCK, kv_width), F32),
+            pltpu.VMEM((width, 3 * col_count), F32),
+        ),
+    )
+    others = head_count - 1
+    chunks = row_count // CHUNK
+    dma = pltpu.SemaphoreType.DMA
+    grad_input, grad_weights = run(
+        exchange_kernel,
+        (),
+        (grads, weight_parts, node_features, x_mine, d_mine, gain_row, gain_mine, w_qkv),
+        (
+            shape((row_count, col_count), BF16),
+            shape((3, share, col_count), F32),
         ),
         scratch=(
             pltpu.VMEM((width, 3 * col_count), BF16),
-            pltpu.VMEM((block_count, BLOCK, kv_width), F32),
-            pltpu.VMEM((width, 3 * col_count), F32),
-        ),
+            pltpu.VMEM((head_count, row_count, col_count), BF16),
+            pltpu.VMEM((others, row_count, col_count), BF16),
+            pltpu.VMEM((block_count, 8, BLOCK), F32),
+            pltpu.VMEM((others, block_count, 8, BLOCK), F32),
+            pltpu.VMEM((seq_count - 1, 3, share, col_count), BF16),
+            dma((others, chunks)),
+            dma((others, chunks)),
+            dma((others,)),
+            dma((others,)),
+            dma((seq_count - 1,)),
+            dma((seq_count - 1,)),
+        ),
+        collective_id=0,
+        has_side_effects=True,
     )
-    row_terms = lax.psum(terms[:, 0, :], "head")
-    grad_parts = lax.all_to_all(grad_parts, "head", split_axis=0, concat_axis=0, tiled=True)
-    weight_parts = lax.all_to_all(weight_parts, "seq", split_axis=0, concat_axis=0, tiled=True)
-    gain_mine = lax.dynamic_slice_in_dim(gain_row, head[0] * col_count, col_count, 1)
-    grad_input = run(
-        input_kernel,
-        (head,),
-        (grad_parts, row_terms, node_features, node_features, d_out, gain_mine),
-        shape((row_count, col_count), BF16),
-        columns=(3, 4),
-        col_count=col_count,
-    )
-    grad_weights = jnp.sum(weight_parts.astype(F32), axis=0)
     return (layer_output, grad_input, grad_weights)
 
 

time: 240 us -> 218 us (0.908)
  blocking collectives: 37.3 us -> 0 us
  Pallas kernels: 35.5 us -> 55.6 us
  starting transfers between devices: 15.7 us -> 11.9 us
    psum x1 -> x0, blocking collectives: 21.5 us -> none  [shards(): row_terms = lax.psum(terms[:, 0, :], 'head')]
    pallas_call x4, Pallas kernels: 35.5 us -> 55.6 us  [run(): pl.pallas_call(kernel, out_shape=outs, grid_spec=pltpu.PrefetchScalarGrid...]
    all_to_all x1 -> x0, blocking collectives: 15.8 us -> none  [shards(): lax.all_to_all(weight_parts, 'seq', split_axis=0, concat_axis=0, tiled=True)]
    all_to_all x1 -> x0, starting transfers between devices: 3.69 us -> none  [shards(): lax.all_to_all(grad_parts, 'head', split_axis=0, concat_axis=0, tiled=True)]
    unnamed x18 -> x22, local copies, waits for them, and re-layouts: 5.22 us -> 5.99 us
  transfers between devices with their start and end apart: 3 -> 2, of which waited for: 2 -> 2; matrix products, arithmetic and copies ran while one was open for 1% -> 1% of each run, Pallas kernels for 0% -> 0%
where the time goes in v2:
time: 218 us
  waiting for transfers between devices  139 us (64%)
  Pallas kernels  55.6 us (26%)
  starting transfers between devices  11.9 us (5%)
  local copies, waits for them, and re-layouts  8.13 us (4%)
    all_to_all x1, waiting for transfers between devices, shards(): lax.all_to_all(returning, 'seq', split_axis=0, concat_axis=0, tiled=True)  69.8 us
    all_to_all x1, waiting for transfers between devices, shards(): lax.all_to_all(outgoing, 'seq', split_axis=0, concat_axis=0, tiled=True)  69.6 us
    pallas_call x4, Pallas kernels, run(): pl.pallas_call(kernel, out_shape=outs, grid_spec=pltpu.PrefetchScalarGrid...  55.6 us
    all_to_all x1, starting transfers between devices, shards(): lax.all_to_all(outgoing, 'seq', split_axis=0, concat_axis=0, tiled=True)  7.28 us
    unnamed x22, local copies, waits for them, and re-layouts  5.99 us
    all_to_all x1, starting transfers between devices, shards(): lax.all_to_all(returning, 'seq', split_axis=0, concat_axis=0, tiled=True)  4.57 us
  transfers between devices with their start and end apart: 2, of which 2 were waited for; matrix products, arithmetic and copies ran while one was open for 1% of the time, Pallas kernels for 0%

profile of v2, /device:TPU:0, one launch (start us, length us, event | category | flops | bytes accessed | tf_op | source)
XLA Modules:
  0.0 217.6 jit_solution(1445902437810338629)
XLA Ops:
  0.7 0.7 add_select_fusion
  1.4 0.1 copy.29
  1.5 0.1 broadcast_in_dim.19
  1.5 0.1 copy.25
  1.6 0.1 reshape.43
  1.7 0.1 copy.26
  1.8 0.0 copy-start.8
  1.8 0.8 convert_reduce_fusion
  2.6 0.1 copy.27
  2.7 0.2 select_reduce_fusion
  2.8 0.1 copy.30
  2.9 0.1 reshape.44.sent_from
  3.0 1.0 copy-done
  4.0 0.7 copy-done.5
  4.7 6.4 %shard_map.85 = (bf16[1536,512]{1,0:T(8,128)(2,1)S(1)}, bf16[1536,128]{1,0:T(8,128)(2,1)S(1)}, bf16[12,128,256]{2,1,0:T(8,128)(2,1)S(1)}, bf16[48,128,256]{2,1,0:T(8,128)(2,1)}) custom-call(s32[48]{0:T(128)S(1)} %reshape.44.sent_from, bf16[1536,512]{1,0:T(8,128)(2,1)} %x_ref.3, f32[1,512]{1,0:T(1,128)S(1)} %bitcast.5, bf16[3,512,128]{2,1,0:T(8,128)(2,1)S(1)} %copy-done), custom_call_target="tpu_custom_call" | custom-call | tf_op jit(solution)/shard_map/pallas_call | solution.py:305
  11.1 1.2 copy-done.2
  12.2 0.7 copy-done.3
  13.0 7.3 %all-to-all-start = ((bf16[48,128,256]{2,1,0:T(8,128)(2,1)}), bf16[48,128,256]{2,1,0:T(8,128)(2,1)}, u32[]{:S(2)}, u32[]{:S(2)}) async-start(bf16[48,128,256]{2,1,0:T(8,128)(2,1)} %get-tuple-element.17), calls=%async_computation | async-start | bytes 6291456 | tf_op jit(solution)/shard_map/all_to_all | solution.py:361
  20.3 1.2 constant_dynamic-slice_fusion
  21.5 69.6 %all-to-all-done.slot_ref = bf16[48,128,256]{2,1,0:T(8,128)(2,1)} async-done(((bf16[48,128,256]{2,1,0:T(8,128)(2,1)}), bf16[48,128,256]{2,1,0:T(8,128)(2,1)}, u32[]{:S(2)}, u32[]{:S(2)}) %all-to-all-start) | async-done | bytes 3145760 | tf_op jit(solution)/shard_map/all_to_all | solution.py:361
  91.1 1.0 copy-done.4
  92.1 16.2 %shard_map.86 = (bf16[1536,128]{1,0:T(8,128)(2,1)}, bf16[1536,128]{1,0:T(8,128)(2,1)S(1)}, f32[12,128,256]{2,1,0:T(8,128)S(1)}, bf16[48,128,256]{2,1,0:T(8,128)(2,1)}) custom-call(s32[36]{0:T(128)S(1)} %fusion.3.slots, s32[12]{0:T(128)S(1)} %copy-done.7, bf16[1536,128]{1,0:T(8,128)(2,1)S(1)} %copy-done.4, ...), custom_call_target="tpu_custom_call" | custom-call | tf_op jit(solution)/shard_map/pallas_call | solution.py:305
  108.3 4.6 %all-to-all-start.1 = ((bf16[48,128,256]{2,1,0:T(8,128)(2,1)}), bf16[48,128,256]{2,1,0:T(8,128)(2,1)}, u32[]{:S(2)}, u32[]{:S(2)}) async-start(bf16[48,128,256]{2,1,0:T(8,128)(2,1)} %get-tuple-element.20), calls=%async_computation.1 | async-start | bytes 6291456 | tf_op jit(solution)/shard_map/all_to_all | solution.py:373
  112.9 0.2 fusion.1
  113.1 0.1 copy.31
  113.2 0.1 reshape.46.filled
  113.3 0.1 dynamic-slice_bitcast_fusion.gain_mine_ref
  113.3 69.8 %all-to-all-done.1.back_ref = bf16[48,128,256]{2,1,0:T(8,128)(2,1)} async-done(((bf16[48,128,256]{2,1,0:T(8,128)(2,1)}), bf16[48,128,256]{2,1,0:T(8,128)(2,1)}, u32[]{:S(2)}, u32[]{:S(2)}) %all-to-all-start.1) | async-done | bytes 3145760 | tf_op jit(solution)/shard_map/all_to_all | solution.py:373
  183.1 6.1 %shard_map.87 = (bf16[1536,384]{1,0:T(8,128)(2,1)S(1)}, bf16[8,3,64,128]{3,2,1,0:T(8,128)(2,1)S(1)}) custom-call(s32[48]{0:T(128)S(1)} %reshape.44.sent_from, s32[48]{0:T(128)S(1)} %reshape.46.filled, f32[12,128,256]{2,1,0:T(8,128)S(1)} %get-tuple-element.19.own_ref, bf16[48,128,256]{2,1,0:T(8,128)(2,1)} %all-to-all-done.1.back_ref, ...), custom_call_target="tpu_custom_call" | custom-call | tf_op jit(solution)/shard_map/pallas_call | solution.py:305
  189.2 26.9 %shard_map.88 = (bf16[1536,128]{1,0:T(8,128)(2,1)S(1)}, f32[3,64,128]{2,1,0:T(8,128)S(1)}) custom-call(bf16[1536,384]{1,0:T(8,128)(2,1)S(1)} %get-tuple-element.23.grads_ref, bf16[8,3,64,128]{3,2,1,0:T(8,128)(2,1)S(1)} %get-tuple-element.24.gw_ref, bf16[1536,512]{1,0:T(8,128)(2,1)} %x_ref.3, bf16[1536,128]{1,0:T(8,128)(2,1)S(1)} %get-tuple-element.29.x_ref.mine_ref, ...), custom_call_target="tpu_custom_call" | custom-call | tf_op jit(solution)/shard_map/pallas_call | solution.py:305
  216.2 0.7 copy.34
  216.9 0.6 copy.35
  (19 shorter events, 0.1 us)
Async XLA Ops:
  1.8 1.2 copy-start.8
  3.0 1.0 copy-start
  4.0 0.7 copy-start.5
  11.1 1.2 copy-start.2
  12.2 0.7 copy-start.3
  13.0 78.1 %all-to-all-start = ((bf16[48,128,256]{2,1,0:T(8,128)(2,1)}), bf16[48,128,256]{2,1,0:T(8,128)(2,1)}, u32[]{:S(2)}, u32[]{:S(2)}) async-start(bf16[48,128,256]{2,1,0:T(8,128)(2,1)} %get-tuple-element.17), calls=%async_computation | async-start | bytes 6291456 | tf_op jit(solution)/shard_map/all_to_all | solution.py:361
  20.3 70.8 %copy-start.7 = (s32[12]{0:T(128)S(1)}, s32[12]{0:T(128)}, u32[]{:S(2)}) copy-start(s32[12]{0:T(128)} %counts.1) | copy-start | bytes 148
  91.1 1.0 copy-start.4
  108.3 4.6 %copy-start.9 = (pred[8,36]{1,0:T(8,128)(4,1)S(1)}, pred[8,36]{1,0:T(8,128)(4,1)}, u32[]{:S(2)}) copy-start(pred[8,36]{1,0:T(8,128)(4,1)} %copy-done.8) | copy-start | bytes 868
  108.3 5.0 %copy-start.6 = (f32[512]{0:T(512)S(1)}, f32[512]{0:T(512)}, u32[]{:S(2)}) copy-start(f32[512]{0:T(512)} %param.7) | copy-start | bytes 6148
  108.3 74.8 %all-to-all-start.1 = ((bf16[48,128,256]{2,1,0:T(8,128)(2,1)}), bf16[48,128,256]{2,1,0:T(8,128)(2,1)}, u32[]{:S(2)}, u32[]{:S(2)}) async-start(bf16[48,128,256]{2,1,0:T(8,128)(2,1)} %get-tuple-element.20), calls=%async_computation.1 | async-start | bytes 6291456 | tf_op jit(solution)/shard_map/all_to_all | solution.py:373
  183.1 6.1 %copy-start.1 = (bf16[3,512,128]{2,1,0:T(8,128)(2,1)S(1)}, bf16[3,512,128]{2,1,0:T(8,128)(2,1)}, u32[]{:S(2)}) copy-start(bf16[3,512,128]{2,1,0:T(8,128)(2,1)} %w_ref.3) | copy-start | bytes 1179652

commit v3 on v2

--- a/solution.py
+++ b/solution.py
@@ -32,9 +32,44 @@
         joined[:, member * cols : (member + 1) * cols] = w_ref[member]
 
 
-def project_kernel(sent_from, x_ref, gain_ref, w_ref, normed_ref, q_ref, kv_ref, out_ref, joined):
+def project_kernel(
+    sent_from,
+    x_ref,
+    gain_ref,
+    w_ref,
+    normed_ref,
+    q_ref,
+    kv_ref,
+    in_ref,
+    joined,
+    relayed,
+    near,
+    far,
+    relay_send,
+    relay_recv,
+    near_send,
+    near_recv,
+    far_send,
+    far_recv,
+    local_sem,
+):
     cols = w_ref.shape[2]
     per_chunk = CHUNK // BLOCK
+    seq_count, capacity = in_ref.shape[:2]
+    half = seq_count // 2
+    seq = lax.axis_index("seq")
+    across = lax.rem(seq + half, seq_count)
+    base = (seq // half) * half
+    mesh_type = pl.DeviceIdType.MESH
+
+    def mate(k):
+        return base + lax.rem(seq - base + k, half)
+
+    barrier = pltpu.get_barrier_semaphore()
+    pl.semaphore_signal(barrier, inc=1, device_id={"seq": across}, device_id_type=mesh_type)
+    for k in range(1, half):
+        pl.semaphore_signal(barrier, inc=1, device_id={"seq": mate(k)}, device_id_type=mesh_type)
+
     join_weights(w_ref, joined, cols)
 
     def project(step, carry):
@@ -51,12 +86,44 @@
         return carry
 
     lax.fori_loop(0, x_ref.shape[0] // CHUNK, project, 0)
-
-    def pack(slot, carry):
-        out_ref[slot] = kv_ref[sent_from[slot]]
-        return carry
-
-    lax.fori_loop(0, out_ref.shape[0], pack, 0)
+    pl.semaphore_wait(barrier, half)
+
+    relay = pltpu.make_async_remote_copy(
+        src_ref=kv_ref,
+        dst_ref=relayed,
+        send_sem=relay_send,
+        recv_sem=relay_recv,
+        device_id={"seq": across},
+        device_id_type=mesh_type,
+    )
+    relay.start()
+
+    def deal(source, which, owner, stage, send, recv):
+        sends = []
+        for k in list(range(1, half)) + [0]:
+            for rank in range(capacity):
+                place = sent_from[(which * seq_count + mate(k)) * capacity + rank]
+                stage[k, rank] = source[place]
+            if k:
+                copy = pltpu.make_async_remote_copy(
+                    src_ref=stage.at[k],
+                    dst_ref=in_ref.at[owner],
+                    send_sem=send.at[k - 1],
+                    recv_sem=recv.at[k - 1],
+                    device_id={"seq": mate(k)},
+                    device_id_type=mesh_type,
+                )
+            else:
+                copy = pltpu.make_async_copy(stage.at[0], in_ref.at[owner], local_sem.at[which])
+            copy.start()
+            sends.append(copy)
+        return sends
+
+    sends = deal(kv_ref, 0, seq, near, near_send, near_recv)
+    relay.wait()
+    sends += deal(relayed, 1, across, far, far_send, far_recv)
+    for copy in sends:
+        copy.wait()
 
 
 def attend_kernel(
@@ -341,24 +408,46 @@
     same = owners[:, :, None] == owners[:, None, :]
     ranks = jnp.sum((same & before[None]).astype(jnp.int32), axis=2)
     places = jnp.arange(capacity, dtype=jnp.int32)
-    picked = (owners[:, None, :] == my_index) & (ranks[:, None, :] == places[None, :, None])
-    sent_from = jnp.sum(jnp.where(picked, in_owner[:, None, :], 0), axis=2).reshape(-1)
-    filled = jnp.any(picked, axis=2).astype(jnp.int32).reshape(-1)
+    half = seq_count // 2
+    holders = jnp.stack([my_index, (my_index + half) % seq_count]).astype(jnp.int32)
+    picked = (owners[None, :, None, :] == holders[:, None, None, None]) & (
+        ranks[None, :, None, :] == places[None, None, :, None]
+    )
+    dealt = jnp.sum(jnp.where(picked, in_owner[None, :, None, :], 0), axis=3)
+    sent_from = dealt[0].reshape(-1)
+    filled = jnp.any(picked[0], axis=2).astype(jnp.int32).reshape(-1)
     my_slots = lax.dynamic_index_in_dim(owners * capacity + ranks, my_index, 0, keepdims=False)
 
-    normed, queries, kv_local, outgoing = run(
+    dma = pltpu.SemaphoreType.DMA
+    vmem = pl.BlockSpec(memory_space=pltpu.VMEM)
+    normed, queries, kv_local, incoming = pl.pallas_call(
         project_kernel,
-        (sent_from,),
-        (node_features, gain_row, w_qkv),
-        (
+        out_shape=(
             shape((row_count, width), BF16),
             shape((row_count, col_count), BF16),
             shape((block_count, BLOCK, kv_width), BF16),
-            shape((slots_all, BLOCK, kv_width), BF16),
-        ),
-        scratch=(pltpu.VMEM((width, 3 * col_count), BF16),),
-    )
-    incoming = lax.all_to_all(outgoing, "seq", split_axis=0, concat_axis=0, tiled=True)
+            shape((seq_count, capacity, BLOCK, kv_width), BF16),
+        ),
+        in_specs=[pl.BlockSpec(memory_space=pltpu.SMEM), vmem, vmem, vmem],
+        out_specs=(vmem, vmem, vmem, pl.BlockSpec(memory_space=pl.ANY)),
+        scratch_shapes=[
+            pltpu.VMEM((width, 3 * col_count), BF16),
+            pltpu.VMEM((block_count, BLOCK, kv_width), BF16),
+            pltpu.VMEM((half, capacity, BLOCK, kv_width), BF16),
+            pltpu.VMEM((half, capacity, BLOCK, kv_width), BF16),
+            dma,
+            dma,
+            dma((half - 1,)),
+            dma((half - 1,)),
+            dma((half - 1,)),
+            dma((half - 1,)),
+            dma((2,)),
+        ],
+        compiler_params=pltpu.CompilerParams(
+            vmem_limit_bytes=VMEM_LIMIT, collective_id=1, has_side_effects=True
+        ),
+    )(dealt.reshape(-1), node_features, gain_row, w_qkv)
+    incoming = incoming.reshape(slots_all, BLOCK, kv_width)
     layer_output, grad_queries, own, returning = run(
         attend_kernel,
         (my_slots, counts),
@@ -387,7 +476,6 @@
     )
     others = head_count - 1
     chunks = row_count // CHUNK
-    dma = pltpu.SemaphoreType.DMA
     grad_input, grad_weights = run(
         exchange_kernel,
         (),

time: 218 us -> 193 us (0.89)
  waiting for transfers between devices: 139 us -> 70.5 us
  Pallas kernels: 55.6 us -> 110 us
  starting transfers between devices: 11.9 us -> 4.45 us
  local copies, waits for them, and re-layouts: 8.13 us -> 4.85 us
    all_to_all x1 -> x0, waiting for transfers between devices: 69.6 us -> none  [shards(): lax.all_to_all(outgoing, 'seq', split_axis=0, concat_axis=0, tiled=True)]
    pallas_call x0 -> x1, Pallas kernels: none -> 60.3 us  [shards(): pl.pallas_call(project_kernel, out_shape=(shape((row_count, width), BF16)...]
    all_to_all x1 -> x0, starting transfers between devices: 7.28 us -> none  [shards(): lax.all_to_all(outgoing, 'seq', split_axis=0, concat_axis=0, tiled=True)]
    pallas_call x4 -> x3, Pallas kernels: 55.6 us -> 49.3 us  [run(): pl.pallas_call(kernel, out_shape=outs, grid_spec=pltpu.PrefetchScalarGrid...]
    unnamed x22 -> x10, local copies, waits for them, and re-layouts: 5.99 us -> 2.54 us
  transfers between devices with their start and end apart: 2 -> 1, of which waited for: 2 -> 1; matrix products, arithmetic and copies ran while one was open for 1% -> 0% of each run, Pallas kernels for 0% -> 0%
where the time goes in v3:
time: 193 us; the launch traced here: 192 us
  Pallas kernels  110 us (57%)
  waiting for transfers between devices  70.5 us (37%)
  local copies, waits for them, and re-layouts  4.85 us (3%)
  starting transfers between devices  4.45 us (2%)
  other arithmetic  2.15 us (1%)
    all_to_all x1, waiting for transfers between devices, shards(): lax.all_to_all(returning, 'seq', split_axis=0, concat_axis=0, tiled=True)  70.5 us
    pallas_call x1, Pallas kernels, shards(): pl.pallas_call(project_kernel, out_shape=(shape((row_count, width), BF16)...  60.3 us
    pallas_call x3, Pallas kernels, run(): pl.pallas_call(kernel, out_shape=outs, grid_spec=pltpu.PrefetchScalarGrid...  49.3 us
    all_to_all x1, starting transfers between devices, shards(): lax.all_to_all(returning, 'seq', split_axis=0, concat_axis=0, tiled=True)  4.45 us
  transfers between devices with their start and end apart: 1, of which 1 were waited for; matrix products, arithmetic and copies ran while one was open for 0% of the time, Pallas kernels for 0%

profile of v3, /device:TPU:0, one launch (start us, length us, event | category | flops | bytes accessed | tf_op | source)
XLA Modules:
  0.0 192.4 jit_solution(10144342697657362786)
XLA Ops:
  0.6 0.0 copy-start
  0.6 0.0 copy-start.2
  0.7 0.7 add_select_fusion
  1.4 0.1 copy.27
  1.5 0.1 reshape.54
  1.6 0.1 copy.28
  1.7 0.8 convert_reduce_fusion
  2.5 0.1 copy.29
  2.6 0.1 copy.31
  2.7 0.1 broadcast_in_dim.20
  2.7 0.1 pad_add_fusion
  2.8 0.1 broadcast_compare_fusion
  2.9 0.3 select_reduce_fusion
  3.2 0.1 copy.32
  3.3 0.1 reshape.55.sent_from
  3.4 0.0 copy-start.3
  3.4 1.2 constant_dynamic-slice_fusion
  4.6 60.3 %shard_map.85 = (bf16[1536,512]{1,0:T(8,128)(2,1)S(1)}, bf16[1536,128]{1,0:T(8,128)(2,1)S(1)}, bf16[12,128,256]{2,1,0:T(8,128)(2,1)S(1)}, bf16[8,6,128,256]{3,2,1,0:T(8,128)(2,1)}) custom-call(s32[96]{0:T(128)S(1)} %reshape.55.sent_from, bf16[1536,512]{1,0:T(8,128)(2,1)} %x_ref.3, f32[1,512]{1,0:T(1,128)S(1)} %bitcast.8, bf16[3,512,128]{2,1,0:T(8,128)(2,1)S(1)} %copy-done), custom_call_target="tpu_custom_call" | custom-call | tf_op jit(solution)/shard_map/pallas_call | solution.py:423
  64.9 1.1 copy-done.1
  66.1 16.3 %shard_map.86 = (bf16[1536,128]{1,0:T(8,128)(2,1)}, bf16[1536,128]{1,0:T(8,128)(2,1)S(1)}, f32[12,128,256]{2,1,0:T(8,128)S(1)}, bf16[48,128,256]{2,1,0:T(8,128)(2,1)}) custom-call(s32[36]{0:T(128)S(1)} %fusion.1.slots, s32[12]{0:T(128)S(1)} %copy-done.3, bf16[1536,128]{1,0:T(8,128)(2,1)S(1)} %get-tuple-element.15.q_ref, ...), custom_call_target="tpu_custom_call" | custom-call | tf_op jit(solution)/shard_map/pallas_call | solution.py:372
  82.4 4.5 %all-to-all-start = ((bf16[48,128,256]{2,1,0:T(8,128)(2,1)}), bf16[48,128,256]{2,1,0:T(8,128)(2,1)}, u32[]{:S(2)}, u32[]{:S(2)}) async-start(bf16[48,128,256]{2,1,0:T(8,128)(2,1)} %get-tuple-element.20), calls=%async_computation | async-start | bytes 6291456 | tf_op jit(solution)/shard_map/all_to_all | solution.py:462
  86.8 0.2 slice_reduce_fusion
  87.0 0.1 copy.34
  87.1 0.1 reshape.58.filled
  87.2 0.1 copy.33
  87.3 0.1 reshape_squeeze.3.sent_from
  87.4 0.1 dynamic-slice_bitcast_fusion.gain_mine_ref
  87.4 70.5 %all-to-all-done.back_ref = bf16[48,128,256]{2,1,0:T(8,128)(2,1)} async-done(((bf16[48,128,256]{2,1,0:T(8,128)(2,1)}), bf16[48,128,256]{2,1,0:T(8,128)(2,1)}, u32[]{:S(2)}, u32[]{:S(2)}) %all-to-all-start) | async-done | bytes 3145760 | tf_op jit(solution)/shard_map/all_to_all | solution.py:462
  158.0 6.1 %shard_map.87 = (bf16[1536,384]{1,0:T(8,128)(2,1)S(1)}, bf16[8,3,64,128]{3,2,1,0:T(8,128)(2,1)S(1)}) custom-call(s32[48]{0:T(128)S(1)} %reshape_squeeze.3.sent_from, s32[48]{0:T(128)S(1)} %reshape.58.filled, f32[12,128,256]{2,1,0:T(8,128)S(1)} %get-tuple-element.19.own_ref, bf16[48,128,256]{2,1,0:T(8,128)(2,1)} %all-to-all-done.back_ref, ...), custom_call_target="tpu_custom_call" | custom-call | tf_op jit(solution)/shard_map/pallas_call | solution.py:372
  164.1 26.9 %shard_map.88 = (bf16[1536,128]{1,0:T(8,128)(2,1)S(1)}, f32[3,64,128]{2,1,0:T(8,128)S(1)}) custom-call(bf16[1536,384]{1,0:T(8,128)(2,1)S(1)} %get-tuple-element.23.grads_ref, bf16[8,3,64,128]{3,2,1,0:T(8,128)(2,1)S(1)} %get-tuple-element.24.gw_ref, bf16[1536,512]{1,0:T(8,128)(2,1)} %x_ref.3, bf16[1536,128]{1,0:T(8,128)(2,1)S(1)} %get-tuple-element.30.x_ref.mine_ref, ...), custom_call_target="tpu_custom_call" | custom-call | tf_op jit(solution)/shard_map/pallas_call | solution.py:372
  191.0 0.7 copy.37
  191.8 0.6 copy.38
  (11 shorter events, 0.1 us)
Async XLA Ops:
  0.6 4.0 %copy-start = (bf16[3,512,128]{2,1,0:T(8,128)(2,1)S(1)}, bf16[3,512,128]{2,1,0:T(8,128)(2,1)}, u32[]{:S(2)}) copy-start(bf16[3,512,128]{2,1,0:T(8,128)(2,1)} %w_ref.3) | copy-start | bytes 1179652
  0.6 4.0 %copy-start.2 = (f32[512]{0:T(512)S(1)}, f32[512]{0:T(512)}, u32[]{:S(2)}) copy-start(f32[512]{0:T(512)} %param.7) | copy-start | bytes 6148
  3.4 62.7 %copy-start.3 = (s32[12]{0:T(128)S(1)}, s32[12]{0:T(128)}, u32[]{:S(2)}) copy-start(s32[12]{0:T(128)} %counts.1) | copy-start | bytes 148
  64.9 1.1 copy-start.1
  82.4 75.6 %all-to-all-start = ((bf16[48,128,256]{2,1,0:T(8,128)(2,1)}), bf16[48,128,256]{2,1,0:T(8,128)(2,1)}, u32[]{:S(2)}, u32[]{:S(2)}) async-start(bf16[48,128,256]{2,1,0:T(8,128)(2,1)} %get-tuple-element.20), calls=%async_computation | async-start | bytes 6291456 | tf_op jit(solution)/shard_map/all_to_all | solution.py:462

commit v4 on v3

--- a/solution.py
+++ b/solution.py
@@ -181,24 +181,130 @@
     lax.fori_loop(0, kv_ref.shape[0], block_step, 0)
 
 
+def return_kernel(
+    far_from,
+    back_ref,
+    near_ref,
+    relay_ref,
+    far_in,
+    summed,
+    far_send,
+    far_recv,
+    near_send,
+    near_recv,
+    relay_send,
+    relay_recv,
+    local_sem,
+):
+    seq_count, capacity = back_ref.shape[:2]
+    block_count = relay_ref.shape[0]
+    half = seq_count // 2
+    piece = BLOCK // 2
+    seq = lax.axis_index("seq")
+    across = lax.rem(seq + half, seq_count)
+    base = (seq // half) * half
+    mesh_type = pl.DeviceIdType.MESH
+
+    def mate(k):
+        return base + lax.rem(seq - base + k, half)
+
+    barrier = pltpu.get_barrier_semaphore()
+    pl.semaphore_signal(barrier, inc=1, device_id={"seq": across}, device_id_type=mesh_type)
+    for k in range(1, half):
+        pl.semaphore_signal(barrier, inc=1, device_id={"seq": mate(k)}, device_id_type=mesh_type)
+    pl.semaphore_wait(barrier, half)
+
+    fars = []
+    nears = []
+    for k in range(1, half):
+        fars.append(
+            pltpu.make_async_remote_copy(
+                src_ref=back_ref.at[lax.rem(mate(k) + half, seq_count)],
+                dst_ref=far_in.at[k - 1],
+                send_sem=far_send.at[k - 1],
+                recv_sem=far_recv.at[k - 1],
+                device_id={"seq": mate(k)},
+                device_id_type=mesh_type,
+            )
+        )
+        nears.append(
+            pltpu.make_async_remote_copy(
+                src_ref=back_ref.at[mate(k)],
+                dst_ref=near_ref.at[k],
+                send_sem=near_send.at[k - 1],
+                recv_sem=near_recv.at[k - 1],
+                device_id={"seq": mate(k)},
+                device_id_type=mesh_type,
+            )
+        )
+    nears.append(pltpu.make_async_copy(back_ref.at[seq], near_ref.at[0], local_sem))
+    for copy in fars:
+        copy.start()
+    for copy in fars:
+        copy.wait()
+    for copy in nears:
+        copy.start()
+
+    def add_block(block, carry):
+        for part in range(2):
+            rows = slice(part * piece, (part + 1) * piece)
+            made = jnp.zeros((piece, back_ref.shape[3]), F32)
+            for k in range(half):
+                for rank in range(capacity):
+                    if k:
+                        term = far_in[k - 1, rank, rows, :]
+                    else:
+                        term = back_ref[across, rank, rows, :]
+                    listed = far_from[k * capacity + rank] == block
+                    made = made + jnp.where(listed, term.astype(F32), 0.0)
+            summed[block, rows, :] = made.astype(BF16)
+        return carry
+
+    lax.fori_loop(0, block_count, add_block, 0)
+    relay = pltpu.make_async_remote_copy(
+        src_ref=summed,
+        dst_ref=relay_ref,
+        send_sem=relay_send,
+        recv_sem=relay_recv,
+        device_id={"seq": across},
+        device_id_type=mesh_type,
+    )
+    relay.start()
+    for copy in nears:
+        copy.wait()
+    relay.wait()
+
+
 def gather_kernel(
-    sent_from, filled, own_ref, back_ref, gq_ref, normed_ref, grads_ref, gw_ref, total, sums, *, node_count
+    near_from,
+    own_ref,
+    near_ref,
+    relay_ref,
+    gq_ref,
+    normed_ref,
+    grads_ref,
+    gw_ref,
+    total,
+    sums,
+    *,
+    node_count,
 ):
     cols = gq_ref.shape[1]
     width = normed_ref.shape[1]
     per_chunk = CHUNK // BLOCK
     sums[...] = jnp.zeros_like(sums)
-    total[...] = own_ref[...]
+    total[...] = own_ref[...] + relay_ref[...].astype(F32)
 
     def gather(slot, carry):
-        @pl.when(filled[slot] > 0)
+        place = near_from[slot]
+
+        @pl.when(place >= 0)
         def _():
-            place = sent_from[slot]
-            total[place] = total[place] + back_ref[slot].astype(F32)
+            total[place] = total[place] + near_ref[slot].astype(F32)
 
         return carry
 
-    lax.fori_loop(0, back_ref.shape[0], gather, 0)
+    lax.fori_loop(0, near_ref.shape[0], gather, 0)
 
     def chunk_step(step, carry):
         rows = rows_of(step, CHUNK)
@@ -408,14 +514,25 @@
     same = owners[:, :, None] == owners[:, None, :]
     ranks = jnp.sum((same & before[None]).astype(jnp.int32), axis=2)
     places = jnp.arange(capacity, dtype=jnp.int32)
+    peers = jnp.arange(seq_count, dtype=jnp.int32)
     half = seq_count // 2
     holders = jnp.stack([my_index, (my_index + half) % seq_count]).astype(jnp.int32)
     picked = (owners[None, :, None, :] == holders[:, None, None, None]) & (
         ranks[None, :, None, :] == places[None, None, :, None]
     )
     dealt = jnp.sum(jnp.where(picked, in_owner[None, :, None, :], 0), axis=3)
-    sent_from = dealt[0].reshape(-1)
-    filled = jnp.any(picked[0], axis=2).astype(jnp.int32).reshape(-1)
+    taken = jnp.where(jnp.any(picked, axis=3), dealt, -1)
+    base = (my_index // half) * half
+    senders = base + (my_index - base - jnp.arange(half, dtype=jnp.int32)) % half
+    near_from, far_from = (
+        jnp.sum(
+            jnp.where(
+                senders[:, None, None] == peers[None, :, None], taken[which][None], 0
+            ),
+            axis=1,
+        ).reshape(-1)
+        for which in range(2)
+    )
     my_slots = lax.dynamic_index_in_dim(owners * capacity + ranks, my_index, 0, keepdims=False)
 
     dma = pltpu.SemaphoreType.DMA
@@ -459,12 +576,36 @@
             shape((slots_all, BLOCK, kv_width), BF16),
         ),
     )
-    returned = lax.all_to_all(returning, "seq", split_axis=0, concat_axis=0, tiled=True)
+    hbm = pl.BlockSpec(memory_space=pl.ANY)
+    near_terms, relay_terms = pl.pallas_call(
+        return_kernel,
+        out_shape=(
+            shape((half, capacity, BLOCK, kv_width), BF16),
+            shape((block_count, BLOCK, kv_width), BF16),
+        ),
+        in_specs=[pl.BlockSpec(memory_space=pltpu.SMEM), vmem],
+        out_specs=(hbm, hbm),
+        scratch_shapes=[
+            pltpu.VMEM((half - 1, capacity, BLOCK, kv_width), BF16),
+            pltpu.VMEM((block_count, BLOCK, kv_width), BF16),
+            dma((half - 1,)),
+            dma((half - 1,)),
+            dma((half - 1,)),
+            dma((half - 1,)),
+            dma,
+            dma,
+            dma,
+        ],
+        compiler_params=pltpu.CompilerParams(
+            vmem_limit_bytes=VMEM_LIMIT, collective_id=2, has_side_effects=True
+        ),
+    )(far_from, returning.reshape(seq_count, capacity, BLOCK, kv_width))
+    near_terms = near_terms.reshape(half * capacity, BLOCK, kv_width)
     share = width // seq_count
     grads, weight_parts = run(
         functools.partial(gather_kernel, node_count=row_count * seq_count),
-        (sent_from, filled),
-        (own, returned, grad_queries, normed),
+        (near_from,),
+        (own, near_terms, relay_terms, grad_queries, normed),
         (
             shape((row_count, 3 * col_count), BF16),
             shape((seq_count, 3, share, col_count), BF16),

time: 193 us -> 180 us (0.933)
  waiting for transfers between devices: 70.5 us -> 0 us
  Pallas kernels: 110 us -> 169 us
  starting transfers between devices: 4.45 us -> 0 us
    all_to_all x1 -> x0, waiting for transfers between devices: 70.5 us -> none  [shards(): lax.all_to_all(returning, 'seq', split_axis=0, concat_axis=0, tiled=True)]
    pallas_call x0 -> x1, Pallas kernels: none -> 61.7 us  [shards(): pl.pallas_call(return_kernel, out_shape=(shape((half, capacity, BLOCK, kv...]
    all_to_all x1 -> x0, starting transfers between devices: 4.45 us -> none  [shards(): lax.all_to_all(returning, 'seq', split_axis=0, concat_axis=0, tiled=True)]
  transfers between devices with their start and end apart: 1 -> 0, of which waited for: 1 -> 0; matrix products, arithmetic and copies ran while one was open for 0% -> 0% of each run, Pallas kernels for 0% -> 0%
where the time goes in v4:
time: 180 us
  Pallas kernels  169 us (94%)
  local copies, waits for them, and re-layouts  6.71 us (4%)
  other arithmetic  2.57 us (1%)
    pallas_call x1, Pallas kernels, shards(): pl.pallas_call(return_kernel, out_shape=(shape((half, capacity, BLOCK, kv...  61.7 us
    pallas_call x1, Pallas kernels, shards(): pl.pallas_call(project_kernel, out_shape=(shape((row_count, width), BF16)...  60.3 us
    pallas_call x3, Pallas kernels, run(): pl.pallas_call(kernel, out_shape=outs, grid_spec=pltpu.PrefetchScalarGrid...  47.5 us
    unnamed x14, local copies, waits for them, and re-layouts  3.68 us

profile of v4, /device:TPU:0, one launch (start us, length us, event | category | flops | bytes accessed | tf_op | source)
XLA Modules:
  0.0 179.6 jit_solution(3313071401570252468)
XLA Ops:
  0.6 0.0 copy-start.4
  0.7 0.1 iota_compare_fusion.2
  0.8 0.1 pad_add_fusion
  0.8 0.8 dynamic-slice_bitcast_fusion.gain_mine_ref
  1.6 0.7 add_select_fusion
  2.3 0.1 copy.39
  2.4 0.1 broadcast_in_dim.61
  2.5 0.1 copy.35
  2.6 0.1 reshape.102
  2.7 0.1 broadcast_compare_fusion
  2.8 0.1 copy.36
  2.8 0.8 convert_reduce_fusion
  3.6 0.1 copy.37
  3.7 0.3 and_reduce_fusion
  4.0 0.3 fusion
  4.3 0.1 copy.40
  4.4 0.1 reshape.103.sent_from
  4.5 0.3 select_reduce_fusion
  4.8 0.1 copy.46
  4.9 0.1 reshape.107.far_from
  5.0 0.1 copy.43
  5.1 0.1 reshape.106.near_from
  5.1 1.2 constant_dynamic-slice_fusion
  6.4 60.3 %shard_map.85 = (bf16[1536,512]{1,0:T(8,128)(2,1)S(1)}, bf16[1536,128]{1,0:T(8,128)(2,1)S(1)}, bf16[12,128,256]{2,1,0:T(8,128)(2,1)S(1)}, bf16[8,6,128,256]{3,2,1,0:T(8,128)(2,1)}) custom-call(s32[96]{0:T(128)S(1)} %reshape.103.sent_from, bf16[1536,512]{1,0:T(8,128)(2,1)} %x_ref.3, f32[1,512]{1,0:T(1,128)S(1)} %bitcast.15, bf16[3,512,128]{2,1,0:T(8,128)(2,1)S(1)} %copy-done), custom_call_target="tpu_custom_call" | custom-call | tf_op jit(solution)/shard_map/pallas_call | solution.py:540
  66.7 1.1 copy-done.1
  67.8 16.3 %shard_map.86 = (bf16[1536,128]{1,0:T(8,128)(2,1)}, bf16[1536,128]{1,0:T(8,128)(2,1)S(1)}, f32[12,128,256]{2,1,0:T(8,128)S(1)}, bf16[48,128,256]{2,1,0:T(8,128)(2,1)}) custom-call(s32[36]{0:T(128)S(1)} %fusion.2.slots, s32[12]{0:T(128)S(1)} %copy-done.5, bf16[1536,128]{1,0:T(8,128)(2,1)S(1)} %get-tuple-element.17.q_ref, ...), custom_call_target="tpu_custom_call" | custom-call | tf_op jit(solution)/shard_map/pallas_call | solution.py:478
  84.1 61.7 %shard_map.87 = (bf16[4,6,128,256]{3,2,1,0:T(8,128)(2,1)S(1)}, bf16[12,128,256]{2,1,0:T(8,128)(2,1)S(1)}) custom-call(s32[24]{0:T(128)S(1)} %reshape.107.far_from, bf16[8,6,128,256]{3,2,1,0:T(8,128)(2,1)} %bitcast.17), custom_call_target="tpu_custom_call" | custom-call | tf_op jit(solution)/shard_map/pallas_call | solution.py:580
  145.8 1.1 copy-done.3
  147.0 5.7 %shard_map.88 = (bf16[1536,384]{1,0:T(8,128)(2,1)S(1)}, bf16[8,3,64,128]{3,2,1,0:T(8,128)(2,1)S(1)}) custom-call(s32[24]{0:T(128)S(1)} %reshape.106.near_from, f32[12,128,256]{2,1,0:T(8,128)} %copy-done.2, bf16[24,128,256]{2,1,0:T(8,128)(2,1)} %bitcast.14, bf16[12,128,256]{2,1,0:T(8,128)(2,1)S(1)} %get-tuple-element.24.relay_ref, ...), custom_call_target="tpu_custom_call" | custom-call | tf_op jit(solution)/shard_map/pallas_call | solution.py:478
  152.7 25.5 %shard_map.89 = (bf16[1536,128]{1,0:T(8,128)(2,1)S(1)}, f32[3,64,128]{2,1,0:T(8,128)S(1)}) custom-call(bf16[1536,384]{1,0:T(8,128)(2,1)S(1)} %get-tuple-element.27.grads_ref, bf16[8,3,64,128]{3,2,1,0:T(8,128)(2,1)S(1)} %get-tuple-element.28.gw_ref, bf16[1536,512]{1,0:T(8,128)(2,1)} %x_ref.3, bf16[1536,128]{1,0:T(8,128)(2,1)S(1)} %get-tuple-element.38.x_ref.mine_ref, ...), custom_call_target="tpu_custom_call" | custom-call | tf_op jit(solution)/shard_map/pallas_call | solution.py:478
  178.2 0.7 copy.51
  178.9 0.6 copy.52
  (16 shorter events, 0.1 us)
Async XLA Ops:
  0.6 5.7 %copy-start = (bf16[3,512,128]{2,1,0:T(8,128)(2,1)S(1)}, bf16[3,512,128]{2,1,0:T(8,128)(2,1)}, u32[]{:S(2)}) copy-start(bf16[3,512,128]{2,1,0:T(8,128)(2,1)} %w_ref.3) | copy-start | bytes 1179652
  0.6 5.7 %copy-start.4 = (f32[512]{0:T(512)S(1)}, f32[512]{0:T(512)}, u32[]{:S(2)}) copy-start(f32[512]{0:T(512)} %param.7) | copy-start | bytes 6148
  5.1 62.7 %copy-start.5 = (s32[12]{0:T(128)S(1)}, s32[12]{0:T(128)}, u32[]{:S(2)}) copy-start(s32[12]{0:T(128)} %counts.1) | copy-start | bytes 148
  66.7 1.1 copy-start.1
  84.1 61.7 %copy-start.2 = (f32[12,128,256]{2,1,0:T(8,128)}, f32[12,128,256]{2,1,0:T(8,128)S(1)}, u32[]{:S(2)}) copy-start(f32[12,128,256]{2,1,0:T(8,128)S(1)} %get-tuple-element.21.own_ref) | copy-start | bytes 4718596
  145.8 1.2 copy-start.3

commit v5 on v4

--- a/solution.py
+++ b/solution.py
@@ -71,6 +71,18 @@
         pl.semaphore_signal(barrier, inc=1, device_id={"seq": mate(k)}, device_id_type=mesh_type)
 
     join_weights(w_ref, joined, cols)
+    pl.semaphore_wait(barrier, half)
+
+    def relay(step):
+        blocks = pl.ds(step * per_chunk, per_chunk)
+        return pltpu.make_async_remote_copy(
+            src_ref=kv_ref.at[blocks],
+            dst_ref=relayed.at[blocks],
+            send_sem=relay_send.at[step],
+            recv_sem=relay_recv.at[step],
+            device_id={"seq": across},
+            device_id_type=mesh_type,
+        )
 
     def project(step, carry):
         rows = rows_of(step, CHUNK)
@@ -83,21 +95,10 @@
         kv_ref[pl.ds(step * per_chunk, per_chunk)] = made[:, cols:].reshape(
             per_chunk, BLOCK, 2 * cols
         )
+        relay(step).start()
         return carry
 
     lax.fori_loop(0, x_ref.shape[0] // CHUNK, project, 0)
-    pl.semaphore_wait(barrier, half)
-
-    relay = pltpu.make_async_remote_copy(
-        src_ref=kv_ref,
-        dst_ref=relayed,
-        send_sem=relay_send,
-        recv_sem=relay_recv,
-        device_id={"seq": across},
-        device_id_type=mesh_type,
-    )
-    relay.start()
-
     def deal(source, which, owner, stage, send, recv):
         sends = []
         for k in list(range(1, half)) + [0]:
@@ -120,7 +121,12 @@
         return sends
 
     sends = deal(kv_ref, 0, seq, near, near_send, near_recv)
-    relay.wait()
+
+    def relay_wait(step, carry):
+        relay(step).wait()
+        return carry
+
+    lax.fori_loop(0, x_ref.shape[0] // CHUNK, relay_wait, 0)
     sends += deal(relayed, 1, across, far, far_send, far_recv)
     for copy in sends:
         copy.wait()
@@ -245,6 +251,16 @@
     for copy in nears:
         copy.start()
 
+    def relay(block):
+        return pltpu.make_async_remote_copy(
+            src_ref=summed.at[block],
+            dst_ref=relay_ref.at[block],
+            send_sem=relay_send.at[block],
+            recv_sem=relay_recv.at[block],
+            device_id={"seq": across},
+            device_id_type=mesh_type,
+        )
+
     def add_block(block, carry):
         for part in range(2):
             rows = slice(part * piece, (part + 1) * piece)
@@ -258,21 +274,17 @@
                     listed = far_from[k * capacity + rank] == block
                     made = made + jnp.where(listed, term.astype(F32), 0.0)
             summed[block, rows, :] = made.astype(BF16)
+        relay(block).start()
+        return carry
+
+    def relay_wait(block, carry):
+        relay(block).wait()
         return carry
 
     lax.fori_loop(0, block_count, add_block, 0)
-    relay = pltpu.make_async_remote_copy(
-        src_ref=summed,
-        dst_ref=relay_ref,
-        send_sem=relay_send,
-        recv_sem=relay_recv,
-        device_id={"seq": across},
-        device_id_type=mesh_type,
-    )
-    relay.start()
     for copy in nears:
         copy.wait()
-    relay.wait()
+    lax.fori_loop(0, block_count, relay_wait, 0)
 
 
 def gather_kernel(
@@ -552,8 +564,8 @@
             pltpu.VMEM((block_count, BLOCK, kv_width), BF16),
             pltpu.VMEM((half, capacity, BLOCK, kv_width), BF16),
             pltpu.VMEM((half, capacity, BLOCK, kv_width), BF16),
-            dma,
-            dma,
+            dma((row_count // CHUNK,)),
+            dma((row_count // CHUNK,)),
             dma((half - 1,)),
             dma((half - 1,)),
             dma((half - 1,)),
@@ -592,8 +604,8 @@
             dma((half - 1,)),
             dma((half - 1,)),
             dma((half - 1,)),
-            dma,
-            dma,
+            dma((block_count,)),
+            dma((block_count,)),
             dma,
         ],
         compiler_params=pltpu.CompilerParams(

time: 180 us -> 178 us (0.989)
  Pallas kernels: 169 us -> 167 us
    pallas_call x1, Pallas kernels: 61.7 us -> 57.1 us  [shards(): pl.pallas_call(return_kernel, out_shape=(shape((half, capacity, BLOCK, kv...]
    pallas_call x3, Pallas kernels: 47.5 us -> 49.3 us  [run(): pl.pallas_call(kernel, out_shape=outs, grid_spec=pltpu.PrefetchScalarGrid...]
where the time goes in v5:
time: 178 us; the launch traced here: 177 us
  Pallas kernels  167 us (94%)
  local copies, waits for them, and re-layouts  6.71 us (4%)
  other arithmetic  2.57 us (1%)
    pallas_call x1, Pallas kernels, shards(): pl.pallas_call(project_kernel, out_shape=(shape((row_count, width), BF16)...  60.9 us
    pallas_call x1, Pallas kernels, shards(): pl.pallas_call(return_kernel, out_shape=(shape((half, capacity, BLOCK, kv...  57.1 us
    pallas_call x3, Pallas kernels, run(): pl.pallas_call(kernel, out_shape=outs, grid_spec=pltpu.PrefetchScalarGrid...  49.3 us
    unnamed x14, local copies, waits for them, and re-layouts  3.68 us

profile of v5, /device:TPU:0, one launch (start us, length us, event | category | flops | bytes accessed | tf_op | source)
XLA Modules:
  0.0 177.4 jit_solution(8760654130954126338)
XLA Ops:
  0.6 0.0 copy-start.4
  0.7 0.1 iota_compare_fusion.2
  0.8 0.1 pad_add_fusion
  0.8 0.8 dynamic-slice_bitcast_fusion.gain_mine_ref
  1.6 0.7 add_select_fusion
  2.3 0.1 copy.39
  2.4 0.1 broadcast_in_dim.61
  2.5 0.1 copy.35
  2.6 0.1 reshape.102
  2.7 0.1 broadcast_compare_fusion
  2.8 0.1 copy.36
  2.8 0.8 convert_reduce_fusion
  3.6 0.1 copy.37
  3.7 0.3 and_reduce_fusion
  4.0 0.3 fusion
  4.3 0.1 copy.40
  4.4 0.1 reshape.103.sent_from
  4.5 0.3 select_reduce_fusion
  4.8 0.1 copy.46
  4.9 0.1 reshape.107.far_from
  5.0 0.1 copy.43
  5.1 0.1 reshape.106.near_from
  5.1 1.2 constant_dynamic-slice_fusion
  6.4 60.9 %shard_map.85 = (bf16[1536,512]{1,0:T(8,128)(2,1)S(1)}, bf16[1536,128]{1,0:T(8,128)(2,1)S(1)}, bf16[12,128,256]{2,1,0:T(8,128)(2,1)S(1)}, bf16[8,6,128,256]{3,2,1,0:T(8,128)(2,1)}) custom-call(s32[96]{0:T(128)S(1)} %reshape.103.sent_from, bf16[1536,512]{1,0:T(8,128)(2,1)} %x_ref.3, f32[1,512]{1,0:T(1,128)S(1)} %bitcast.15, bf16[3,512,128]{2,1,0:T(8,128)(2,1)S(1)} %copy-done), custom_call_target="tpu_custom_call" | custom-call | tf_op jit(solution)/shard_map/pallas_call | solution.py:552
  67.2 1.1 copy-done.1
  68.4 16.3 %shard_map.86 = (bf16[1536,128]{1,0:T(8,128)(2,1)}, bf16[1536,128]{1,0:T(8,128)(2,1)S(1)}, f32[12,128,256]{2,1,0:T(8,128)S(1)}, bf16[48,128,256]{2,1,0:T(8,128)(2,1)}) custom-call(s32[36]{0:T(128)S(1)} %fusion.2.slots, s32[12]{0:T(128)S(1)} %copy-done.5, bf16[1536,128]{1,0:T(8,128)(2,1)S(1)} %get-tuple-element.17.q_ref, ...), custom_call_target="tpu_custom_call" | custom-call | tf_op jit(solution)/shard_map/pallas_call | solution.py:490
  84.6 57.1 %shard_map.87 = (bf16[4,6,128,256]{3,2,1,0:T(8,128)(2,1)S(1)}, bf16[12,128,256]{2,1,0:T(8,128)(2,1)S(1)}) custom-call(s32[24]{0:T(128)S(1)} %reshape.107.far_from, bf16[8,6,128,256]{3,2,1,0:T(8,128)(2,1)} %bitcast.17), custom_call_target="tpu_custom_call" | custom-call | tf_op jit(solution)/shard_map/pallas_call | solution.py:592
  141.8 1.1 copy-done.3
  142.9 5.7 %shard_map.88 = (bf16[1536,384]{1,0:T(8,128)(2,1)S(1)}, bf16[8,3,64,128]{3,2,1,0:T(8,128)(2,1)S(1)}) custom-call(s32[24]{0:T(128)S(1)} %reshape.106.near_from, f32[12,128,256]{2,1,0:T(8,128)} %copy-done.2, bf16[24,128,256]{2,1,0:T(8,128)(2,1)} %bitcast.14, bf16[12,128,256]{2,1,0:T(8,128)(2,1)S(1)} %get-tuple-element.24.relay_ref, ...), custom_call_target="tpu_custom_call" | custom-call | tf_op jit(solution)/shard_map/pallas_call | solution.py:490
  148.6 27.4 %shard_map.89 = (bf16[1536,128]{1,0:T(8,128)(2,1)S(1)}, f32[3,64,128]{2,1,0:T(8,128)S(1)}) custom-call(bf16[1536,384]{1,0:T(8,128)(2,1)S(1)} %get-tuple-element.27.grads_ref, bf16[8,3,64,128]{3,2,1,0:T(8,128)(2,1)S(1)} %get-tuple-element.28.gw_ref, bf16[1536,512]{1,0:T(8,128)(2,1)} %x_ref.3, bf16[1536,128]{1,0:T(8,128)(2,1)S(1)} %get-tuple-element.38.x_ref.mine_ref, ...), custom_call_target="tpu_custom_call" | custom-call | tf_op jit(solution)/shard_map/pallas_call | solution.py:490
  176.0 0.7 copy.51
  176.7 0.6 copy.52
  (16 shorter events, 0.1 us)
Async XLA Ops:
  0.6 5.7 %copy-start = (bf16[3,512,128]{2,1,0:T(8,128)(2,1)S(1)}, bf16[3,512,128]{2,1,0:T(8,128)(2,1)}, u32[]{:S(2)}) copy-start(bf16[3,512,128]{2,1,0:T(8,128)(2,1)} %w_ref.3) | copy-start | bytes 1179652
  0.6 5.7 %copy-start.4 = (f32[512]{0:T(512)S(1)}, f32[512]{0:T(512)}, u32[]{:S(2)}) copy-start(f32[512]{0:T(512)} %param.7) | copy-start | bytes 6148
  5.1 63.2 %copy-start.5 = (s32[12]{0:T(128)S(1)}, s32[12]{0:T(128)}, u32[]{:S(2)}) copy-start(s32[12]{0:T(128)} %counts.1) | copy-start | bytes 148
  67.2 1.1 copy-start.1
  84.6 57.1 %copy-start.2 = (f32[12,128,256]{2,1,0:T(8,128)}, f32[12,128,256]{2,1,0:T(8,128)S(1)}, u32[]{:S(2)}) copy-start(f32[12,128,256]{2,1,0:T(8,128)S(1)} %get-tuple-element.21.own_ref) | copy-start | bytes 4718596
  141.8 1.2 copy-start.3

commit v6 on v5

--- a/solution.py
+++ b/solution.py
@@ -184,7 +184,7 @@
             )
         return carry
 
-    lax.fori_loop(0, kv_ref.shape[0], block_step, 0)
+    lax.fori_loop(0, kv_ref.shape[0], block_step, 0, unroll=2)
 
 
 def return_kernel(

time: 178 us -> 177 us (level)
  no operation moved by 1% of the time
where the time goes in v6:
time: 177 us
  Pallas kernels  166 us (94%)
  local copies, waits for them, and re-layouts  6.71 us (4%)
  other arithmetic  2.57 us (1%)
    pallas_call x1, Pallas kernels, shards(): pl.pallas_call(project_kernel, out_shape=(shape((row_count, width), BF16)...  60.9 us
    pallas_call x1, Pallas kernels, shards(): pl.pallas_call(return_kernel, out_shape=(shape((half, capacity, BLOCK, kv...  57.1 us
    pallas_call x3, Pallas kernels, run(): pl.pallas_call(kernel, out_shape=outs, grid_spec=pltpu.PrefetchScalarGrid...  48.5 us
    unnamed x14, local copies, waits for them, and re-layouts  3.68 us

profile of v6, /device:TPU:0, one launch (start us, length us, event | category | flops | bytes accessed | tf_op | source)
XLA Modules:
  0.0 176.6 jit_solution(4601849838008399424)
XLA Ops:
  0.6 0.0 copy-start.4
  0.7 0.1 iota_compare_fusion.2
  0.8 0.1 pad_add_fusion
  0.8 0.8 dynamic-slice_bitcast_fusion.gain_mine_ref
  1.6 0.7 add_select_fusion
  2.3 0.1 copy.39
  2.4 0.1 broadcast_in_dim.61
  2.5 0.1 copy.35
  2.6 0.1 reshape.102
  2.7 0.1 broadcast_compare_fusion
  2.8 0.1 copy.36
  2.8 0.8 convert_reduce_fusion
  3.6 0.1 copy.37
  3.7 0.3 and_reduce_fusion
  4.0 0.3 fusion
  4.3 0.1 copy.40
  4.4 0.1 reshape.103.sent_from
  4.5 0.3 select_reduce_fusion
  4.8 0.1 copy.46
  4.9 0.1 reshape.107.far_from
  5.0 0.1 copy.43
  5.1 0.1 reshape.106.near_from
  5.1 1.2 constant_dynamic-slice_fusion
  6.4 60.9 %shard_map.85 = (bf16[1536,512]{1,0:T(8,128)(2,1)S(1)}, bf16[1536,128]{1,0:T(8,128)(2,1)S(1)}, bf16[12,128,256]{2,1,0:T(8,128)(2,1)S(1)}, bf16[8,6,128,256]{3,2,1,0:T(8,128)(2,1)}) custom-call(s32[96]{0:T(128)S(1)} %reshape.103.sent_from, bf16[1536,512]{1,0:T(8,128)(2,1)} %x_ref.3, f32[1,512]{1,0:T(1,128)S(1)} %bitcast.15, bf16[3,512,128]{2,1,0:T(8,128)(2,1)S(1)} %copy-done), custom_call_target="tpu_custom_call" | custom-call | tf_op jit(solution)/shard_map/pallas_call | solution.py:552
  67.2 1.1 copy-done.1
  68.4 15.4 %shard_map.86 = (bf16[1536,128]{1,0:T(8,128)(2,1)}, bf16[1536,128]{1,0:T(8,128)(2,1)S(1)}, f32[12,128,256]{2,1,0:T(8,128)S(1)}, bf16[48,128,256]{2,1,0:T(8,128)(2,1)}) custom-call(s32[36]{0:T(128)S(1)} %fusion.2.slots, s32[12]{0:T(128)S(1)} %copy-done.5, bf16[1536,128]{1,0:T(8,128)(2,1)S(1)} %get-tuple-element.17.q_ref, ...), custom_call_target="tpu_custom_call" | custom-call | tf_op jit(solution)/shard_map/pallas_call | solution.py:490
  83.8 57.1 %shard_map.87 = (bf16[4,6,128,256]{3,2,1,0:T(8,128)(2,1)S(1)}, bf16[12,128,256]{2,1,0:T(8,128)(2,1)S(1)}) custom-call(s32[24]{0:T(128)S(1)} %reshape.107.far_from, bf16[8,6,128,256]{3,2,1,0:T(8,128)(2,1)} %bitcast.17), custom_call_target="tpu_custom_call" | custom-call | tf_op jit(solution)/shard_map/pallas_call | solution.py:592
  140.9 1.1 copy-done.3
  142.1 5.7 %shard_map.88 = (bf16[1536,384]{1,0:T(8,128)(2,1)S(1)}, bf16[8,3,64,128]{3,2,1,0:T(8,128)(2,1)S(1)}) custom-call(s32[24]{0:T(128)S(1)} %reshape.106.near_from, f32[12,128,256]{2,1,0:T(8,128)} %copy-done.2, bf16[24,128,256]{2,1,0:T(8,128)(2,1)} %bitcast.14, bf16[12,128,256]{2,1,0:T(8,128)(2,1)S(1)} %get-tuple-element.24.relay_ref, ...), custom_call_target="tpu_custom_call" | custom-call | tf_op jit(solution)/shard_map/pallas_call | solution.py:490
  147.8 27.4 %shard_map.89 = (bf16[1536,128]{1,0:T(8,128)(2,1)S(1)}, f32[3,64,128]{2,1,0:T(8,128)S(1)}) custom-call(bf16[1536,384]{1,0:T(8,128)(2,1)S(1)} %get-tuple-element.27.grads_ref, bf16[8,3,64,128]{3,2,1,0:T(8,128)(2,1)S(1)} %get-tuple-element.28.gw_ref, bf16[1536,512]{1,0:T(8,128)(2,1)} %x_ref.3, bf16[1536,128]{1,0:T(8,128)(2,1)S(1)} %get-tuple-element.38.x_ref.mine_ref, ...), custom_call_target="tpu_custom_call" | custom-call | tf_op jit(solution)/shard_map/pallas_call | solution.py:490
  175.2 0.7 copy.51
  175.9 0.6 copy.52
  (16 shorter events, 0.1 us)
Async XLA Ops:
  0.6 5.7 %copy-start = (bf16[3,512,128]{2,1,0:T(8,128)(2,1)S(1)}, bf16[3,512,128]{2,1,0:T(8,128)(2,1)}, u32[]{:S(2)}) copy-start(bf16[3,512,128]{2,1,0:T(8,128)(2,1)} %w_ref.3) | copy-start | bytes 1179652
  0.6 5.7 %copy-start.4 = (f32[512]{0:T(512)S(1)}, f32[512]{0:T(512)}, u32[]{:S(2)}) copy-start(f32[512]{0:T(512)} %param.7) | copy-start | bytes 6148
  5.1 63.2 %copy-start.5 = (s32[12]{0:T(128)S(1)}, s32[12]{0:T(128)}, u32[]{:S(2)}) copy-start(s32[12]{0:T(128)} %counts.1) | copy-start | bytes 148
  67.2 1.1 copy-start.1
  83.8 57.1 %copy-start.2 = (f32[12,128,256]{2,1,0:T(8,128)}, f32[12,128,256]{2,1,0:T(8,128)S(1)}, u32[]{:S(2)}) copy-start(f32[12,128,256]{2,1,0:T(8,128)S(1)} %get-tuple-element.21.own_ref) | copy-start | bytes 4718596
  140.9 1.2 copy-start.3
